TPU v7x, 512 devices: a whole 4x8x8 slice. The times are simulated.
512 devices in a mesh: rows: 128 (over y, z, core), rep: 4 (over x).
Axes of the slice: x: 4, y: 8, z: 8, core: 2. Of those that a mesh axis runs over, the one named last changes fastest.
Arguments:
- embeddings: bfloat16 [32768, 1024], P('rows', 'rep'), may hold values from -6 to 6
- coarse_ids: int32 [32768], P('rows'), may hold values from 0 to 255
- fine_ids: int32 [32768], P('rows'), may hold values from 0 to 65535, as said below
- pq_codes: int32 [32768, 64], P('rows', 'rep'), may hold values from 0 to 255
- old_coarse: float32 [256, 1024], P(None, 'rep'), may hold values from -3 to 3
- old_fine: float32 [65536, 1024], P('rows', 'rep'), may hold values from -3 to 3
- old_codebook: float32 [256, 1024], P('rows', 'rep'), may hold values from -3 to 3
Outputs:
- new_coarse: float32 [256, 1024], P(None, 'rep')
- new_fine: float32 [65536, 1024], P('rows', 'rep')
- residual: bfloat16 [32768, 1024], P('rows', 'rep')
- new_codebook: float32 [256, 1024], P('rows', 'rep')
- row_error: float32 [32768], P('rows')
Inputs may be any that keep to these rules, and one draw needn't show every extreme that they name: `fine_ids`: within each aligned block of 256 rows, at most 8 ids lie in any one range o * 512 to (o + 1) * 512 - 1, and in every block some range holds exactly 8 of them.
All inputs are finite; a program needn't handle non-finite values.
Results may differ from a plain program's by a relative error of at most 0.0049.
Values may be sent and summed in bfloat16 or wider, within the bound.
A program may use at most 64 MiB of HBM per device.

v0:
```python
import math

import jax
import jax.numpy as jnp
from jax import lax
from jax.sharding import Mesh
from jax.sharding import PartitionSpec as P

ROWS = ("rows_0", "rows_1", "rows_2")


def filled_up(lines, count):
    spare = -len(lines) % count
    return jnp.pad(lines, [(0, spare)] + [(0, 0)] * (lines.ndim - 1))


def copy_for_each(shard, axis):
    count = lax.axis_size(axis)
    return lax.all_to_all(
        jnp.broadcast_to(shard[None], (count, *shard.shape)), axis, 0, 0, tiled=True
    )


def joined_along(tiles, dim):
    tiles = jnp.moveaxis(tiles, 0, dim)
    shape = tiles.shape
    return tiles.reshape(*shape[:dim], shape[dim] * shape[dim + 1], *shape[dim + 2 :])


def whole_of(shard, axes, dim):
    far, near = axes
    tiles = copy_for_each(copy_for_each(shard, far), near)
    return joined_along(tiles.swapaxes(0, 1).reshape(-1, *shard.shape), dim)


def cut_along(shard, dim, count):
    before, after = (shard.shape[:dim], shard.shape[dim + 1 :])
    return jnp.moveaxis(shard.reshape(*before, count, -1, *after), dim, 0)


def summed_on_arrival(shard, axis, dim):
    count = lax.axis_size(axis)
    tiles = lax.all_to_all(cut_along(shard, dim, count), axis, 0, 0, tiled=True)
    return jnp.sum(tiles, axis=0)


def sum_in_two_steps(shard, axes, dim):
    far, near = axes
    own = summed_on_arrival(cut_along(shard, dim, lax.axis_size(far)), near, dim + 1)
    return jnp.sum(lax.all_to_all(own, far, 0, 0, tiled=True), axis=0)


def total_of(shard, axes):
    padded = filled_up(shard, lax.axis_size(axes[0]) * lax.axis_size(axes[1]))
    whole = whole_of(sum_in_two_steps(padded, axes, 0), axes, 0)
    return lax.slice_in_dim(whole, 0, len(shard)).reshape(shard.shape)


def packed_total(arrays, axis):
    vector, at, outs = (jnp.concatenate([a.reshape(-1) for a in arrays]), 0, [])
    subtotal = total_of(vector, axis)
    for a in arrays:
        outs.append(subtotal[at : at + a.size].reshape(a.shape))
        at += a.size
    return tuple(outs)


def over_copies(shard, axis):
    everything = copy_for_each(shard, axis)
    return jnp.sum(everything, axis=0)


def update_means(sums, counts, fallback):
    return jnp.where(counts[:, None] > 0, sums / jnp.maximum(counts, 1.0)[:, None], fallback)


def shards(embeddings, coarse_ids, fine_ids, pq_codes, old_coarse, old_fine, old_codebook):
    owner_rows = lax.axis_size(ROWS)
    row_total, width_dev = embeddings.shape
    coarse_total = old_coarse.shape[0]
    coarse_hot = coarse_ids[None, :] == jnp.arange(coarse_total, dtype=jnp.int32)[:, None]
    coarse_sum = jnp.dot(
        coarse_hot.astype(jnp.bfloat16), embeddings, preferred_element_type=jnp.float32
    )
    coarse_count = jnp.sum(coarse_hot, axis=1).astype(jnp.float32)
    coarse_sum, coarse_count = packed_total(
        (coarse_sum, coarse_count), (("rows_0", "rows_1"), "rows_2")
    )
    new_coarse = update_means(coarse_sum, coarse_count, old_coarse)
    coarse_residual = (
        embeddings.astype(jnp.float32) - jnp.take(new_coarse, coarse_ids, axis=0)
    ).astype(jnp.bfloat16)
    fine_dev = old_fine.shape[0]
    capacity = 4 * row_total // owner_rows
    slot_total = owner_rows * capacity
    owner_ids = fine_ids // fine_dev
    local_ids = fine_ids % fine_dev
    owner_hot = (owner_ids[:, None] == jnp.arange(owner_rows, dtype=jnp.int32)[None, :]).astype(
        jnp.int32
    )
    rank_in = jnp.sum(jnp.cumsum(owner_hot, axis=0) * owner_hot, axis=1) - 1
    slot_of_row = owner_ids * capacity + rank_in
    row_of_slot = (
        jnp.full((slot_total,), row_total, jnp.int32)
        .at[slot_of_row]
        .set(jnp.arange(row_total, dtype=jnp.int32))
    )
    send_rows = jnp.take(coarse_residual, row_of_slot, axis=0, mode="fill", fill_value=0).reshape(
        owner_rows, capacity, width_dev
    )
    send_ids = (
        jnp.full((slot_total,), -1, jnp.int32)
        .at[slot_of_row]
        .set(local_ids)
        .reshape(owner_rows, capacity)
    )
    recv_rows, recv_ids = (
        lax.all_to_all(send_rows, ROWS, split_axis=0, concat_axis=0, tiled=True),
        lax.all_to_all(send_ids, ROWS, split_axis=0, concat_axis=0, tiled=True),
    )
    rows_flat = recv_rows.reshape(slot_total, width_dev)
    ids_flat = recv_ids.reshape(slot_total)
    block_size = math.gcd(slot_total, 2048)
    fine_range = jnp.arange(fine_dev, dtype=jnp.int32)

    def fine_step(running, pieces):
        sums, counts = running
        block_rows, block_ids = pieces
        one_hot = block_ids[None, :] == fine_range[:, None]
        sums = sums + jnp.dot(
            one_hot.astype(jnp.bfloat16), block_rows, preferred_element_type=jnp.float32
        )
        counts = counts + jnp.sum(one_hot, axis=1).astype(jnp.float32)
        return ((sums, counts), None)

    start_fine = (
        jnp.zeros((fine_dev, width_dev), jnp.float32),
        jnp.zeros((fine_dev,), jnp.float32),
    )
    (fine_sum, fine_count), _ = lax.scan(
        fine_step,
        start_fine,
        (
            rows_flat.reshape(slot_total // block_size, block_size, width_dev),
            ids_flat.reshape(slot_total // block_size, block_size),
        ),
    )
    new_fine = update_means(fine_sum, fine_count, old_fine)
    safe_ids = jnp.maximum(ids_flat, 0)
    at_owner = (rows_flat.astype(jnp.float32) - jnp.take(new_fine, safe_ids, axis=0)).astype(
        jnp.bfloat16
    )
    returned = lax.all_to_all(
        at_owner.reshape(owner_rows, capacity, width_dev),
        ROWS,
        split_axis=0,
        concat_axis=0,
        tiled=True,
    ).reshape(slot_total, width_dev)
    residual = jnp.take(returned, slot_of_row, axis=0)
    sub_dev = pq_codes.shape[1]
    sub_width = width_dev // sub_dev
    share_codes = old_codebook.shape[0]
    book_rows = share_codes * owner_rows
    code_block = math.gcd(row_total, 512)
    code_range = jnp.arange(book_rows, dtype=jnp.int32)

    def code_step(running, pieces):
        sums, counts = running
        block_rows, block_codes = pieces
        one_hot = block_codes.T[:, None, :] == code_range[None, :, None]
        split_rows = block_rows.reshape(code_block, sub_dev, sub_width)
        sums = sums + jnp.einsum(
            "mkn,nmd->kmd",
            one_hot.astype(jnp.bfloat16),
            split_rows,
            preferred_element_type=jnp.float32,
        )
        counts = counts + jnp.sum(one_hot, axis=2).T.astype(jnp.float32)
        return ((sums, counts), None)

    start_code = (
        jnp.zeros((book_rows, sub_dev, sub_width), jnp.float32),
        jnp.zeros((book_rows, sub_dev), jnp.float32),
    )
    (code_sum, code_count), _ = lax.scan(
        code_step,
        start_code,
        (
            residual.reshape(row_total // code_block, code_block, width_dev),
            pq_codes.reshape(row_total // code_block, code_block, sub_dev),
        ),
    )
    code_sum = code_sum.reshape(book_rows, width_dev)
    code_sum, code_count = packed_total((code_sum, code_count), (("rows_0", "rows_1"), "rows_2"))
    column_count = jnp.repeat(code_count, sub_width, axis=1)
    averages = code_sum / jnp.maximum(column_count, 1.0)
    first_code = lax.axis_index(ROWS) * share_codes
    own_count = lax.dynamic_slice_in_dim(column_count, first_code, share_codes, 0)
    own_average = lax.dynamic_slice_in_dim(averages, first_code, share_codes, 0)
    new_codebook = jnp.where(own_count > 0, own_average, old_codebook)
    book_view = averages.reshape(book_rows, sub_dev, sub_width)
    rebuilt = book_view[pq_codes, jnp.arange(sub_dev, dtype=jnp.int32)[None, :]].reshape(
        row_total, width_dev
    )
    differ = residual.astype(jnp.float32) - rebuilt
    partial_error = jnp.sum(differ * differ, axis=1)
    row_error = over_copies(partial_error, "rep") / (width_dev * lax.axis_size("rep"))
    return (new_coarse, new_fine, residual, new_codebook, row_error)


def solution(mesh):
    torus = Mesh(
        mesh.devices.reshape(8, 8, 2, mesh.shape["rep"]), ("rows_0", "rows_1", "rows_2", "rep")
    )
    placed = (
        P(ROWS, "rep"),
        P(ROWS),
        P(ROWS),
        P(ROWS, "rep"),
        P(None, "rep"),
        P(ROWS, "rep"),
        P(ROWS, "rep"),
    )
    return jax.shard_map(
        shards,
        mesh=torus,
        in_specs=placed,
        out_specs=(P(None, "rep"), P(ROWS, "rep"), P(ROWS, "rep"), P(ROWS, "rep"), P(ROWS)),
        check_vma=False,
    )
```

profile of v0, /device:TPU:1, one launch (start us, length us, event | category | flops | bytes accessed | tf_op | source)
XLA Modules:
  0.0 254.6 jit_solution(14182597078314242246)
XLA Ops:
  0.6 0.8 convert_reduce_fusion.2
  1.4 1.1 convolution_bitcast_fusion
  2.6 0.1 copy.115
  2.8 0.4 reshape_reshape.15
  3.2 10.5 %all_to_all.75 = f32[2,64,514]{2,1,0:T(8,128)S(1)} all-to-all(f32[2,64,514]{2,1,0:T(8,128)S(1)} %copy.89), channel_id=1, replica_groups=mesh['rows_0'=8,'rows_1'=8,'rows_2'=2,'rep'=4] {'rows_2'}, dimensions={0} | all-to-all | bytes 526336 | tf_op jit(solution)/shard_map/all_to_all | solution.py:43
  13.7 0.8 all_to_all.49
  14.5 10.9 %all-to-all-start.1 = ((f32[64,1,514]{2,1,0:T(1,128)}), f32[64,1,514]{2,1,0:T(1,128)S(1)}, u32[]{:S(2)}, u32[]{:S(2)}) async-start(f32[64,1,514]{2,1,0:T(1,128)} %all_to_all.49), calls=%async_computation.1 | async-start | bytes 327680 | tf_op jit(solution)/shard_map/all_to_all | solution.py:50
  25.6 0.2 fusion.11
  25.9 0.2 fusion.12
  26.1 1.4 scatter_custom_fusion
  27.5 0.7 all_to_all.53
  28.2 1.4 scatter_custom_fusion.1
  29.7 7.5 %all-to-all-done.1 = f32[64,1,514]{2,1,0:T(1,128)S(1)} async-done(((f32[64,1,514]{2,1,0:T(1,128)}), f32[64,1,514]{2,1,0:T(1,128)S(1)}, u32[]{:S(2)}, u32[]{:S(2)}) %all-to-all-start.1) | async-done | bytes 131616 | tf_op jit(solution)/shard_map/all_to_all | solution.py:50
  37.1 7.7 %all-to-all-start.4 = ((s32[128,1,8]{2,1,0:T(1,128)}), s32[128,1,8]{2,1,0:T(1,128)S(1)}, u32[]{:S(2)}, u32[]{:S(2)}) async-start(s32[128,1,8]{2,1,0:T(1,128)} %bitcast.6), calls=%async_computation.4 | async-start | bytes 131072 | tf_op jit(solution)/shard_map/all_to_all | solution.py:119
  44.9 0.1 reduce_sum.94
  45.0 11.5 %all-to-all-done.4 = s32[128,1,8]{2,1,0:T(1,128)S(1)} async-done(((s32[128,1,8]{2,1,0:T(1,128)}), s32[128,1,8]{2,1,0:T(1,128)S(1)}, u32[]{:S(2)}, u32[]{:S(2)}) %all-to-all-start.4) | async-done | bytes 4128 | tf_op jit(solution)/shard_map/all_to_all | solution.py:119
  56.5 0.8 broadcast_in_dim.141
  57.3 4.6 %all-to-all-start.2 = ((f32[64,1,514]{2,1,0:T(1,128)}), f32[64,1,514]{2,1,0:T(1,128)S(1)}, u32[]{:S(2)}, u32[]{:S(2)}) async-start(f32[64,1,514]{2,1,0:T(1,128)} %broadcast_in_dim.141), calls=%async_computation.2 | async-start | bytes 327680 | tf_op jit(solution)/shard_map/all_to_all | solution.py:19
  62.1 11.5 %all-to-all-done.2 = f32[64,1,514]{2,1,0:T(1,128)S(1)} async-done(((f32[64,1,514]{2,1,0:T(1,128)}), f32[64,1,514]{2,1,0:T(1,128)S(1)}, u32[]{:S(2)}, u32[]{:S(2)}) %all-to-all-start.2) | async-done | bytes 131616 | tf_op jit(solution)/shard_map/all_to_all | solution.py:19
  73.6 6.2 %all_to_all.76 = f32[2,64,514]{2,1,0:T(8,128)S(1)} all-to-all(f32[2,64,514]{2,1,0:T(8,128)S(1)} %broadcast_in_dim.143), channel_id=1, replica_groups=mesh['rows_0'=8,'rows_1'=8,'rows_2'=2,'rep'=4] {'rows_2'}, dimensions={0} | all-to-all | bytes 526336 | tf_op jit(solution)/shard_map/all_to_all | solution.py:19
  79.8 0.3 copy.90
  80.0 0.4 reshape_reshape.16
  80.4 0.5 slice.28
  80.9 0.1 fusion.10
  81.1 1.0 gather_fusion
  82.2 3.9 %gather_fusion.1 = bf16[1024,256]{1,0:T(8,128)(2,1)S(1)} fusion(bf16[256,256]{1,0:T(8,128)(2,1)S(1)} %subtract_convert_fusion, s32[1024]{0:T(1024)S(1)} %fusion.23), kind=kCustom, calls=%fused_computation.1 | custom fusion | bytes 1052672 | tf_op jit(solution)/shard_map/jit(_take)/gather | solution.py:108
  86.2 1.0 bitcast_select_fusion.1
  87.2 5.7 %all-to-all-start.5 = ((bf16[128,8,256]{2,1,0:T(8,128)(2,1)}), bf16[128,8,256]{2,1,0:T(8,128)(2,1)S(1)}, u32[]{:S(2)}, u32[]{:S(2)}) async-start(bf16[128,8,256]{2,1,0:T(8,128)(2,1)} %bitcast_select_fusion.1), calls=%async_computation.5 | async-start | bytes 1048576 | tf_op jit(solution)/shard_map/all_to_all | solution.py:118
  92.9 0.5 broadcast.202
  93.4 0.8 reduce.10
  94.7 0.3 convert_reduce_fusion.1
  95.0 17.5 %all-to-all-done.5 = bf16[128,8,256]{2,1,0:T(8,128)(2,1)S(1)} async-done(((bf16[128,8,256]{2,1,0:T(8,128)(2,1)}), bf16[128,8,256]{2,1,0:T(8,128)(2,1)S(1)}, u32[]{:S(2)}, u32[]{:S(2)}) %all-to-all-start.5) | async-done | bytes 524320 | tf_op jit(solution)/shard_map/all_to_all | solution.py:118
  112.5 0.5 fusion.4
  113.0 3.5 %gather_fusion.2 = f32[1024,256]{1,0:T(8,128)S(1)} fusion(f32[512,256]{1,0:T(8,128)S(1)} %fusion.4, s32[1024]{0:T(1024)S(1)} %broadcast_clamp_fusion), kind=kCustom, calls=%fused_computation.2 | custom fusion | bytes 2101248 | tf_op jit(solution)/shard_map/jit(_take)/gather | solution.py:150
  116.5 1.0 fusion.7
  117.5 7.1 %all-to-all-start.6 = ((bf16[128,8,256]{2,1,0:T(8,128)(2,1)}), bf16[128,8,256]{2,1,0:T(8,128)(2,1)S(1)}, u32[]{:S(2)}, u32[]{:S(2)}) async-start(bf16[128,8,256]{2,1,0:T(8,128)(2,1)} %fusion.7), calls=%async_computation.6 | async-start | bytes 1048576 | tf_op jit(solution)/shard_map/all_to_all | solution.py:153
  124.6 0.6 convert_reduce_fusion
  125.5 18.7 %all-to-all-done.6 = bf16[128,8,256]{2,1,0:T(8,128)(2,1)S(1)} async-done(((bf16[128,8,256]{2,1,0:T(8,128)(2,1)}), bf16[128,8,256]{2,1,0:T(8,128)(2,1)S(1)}, u32[]{:S(2)}, u32[]{:S(2)}) %all-to-all-start.6) | async-done | bytes 524320 | tf_op jit(solution)/shard_map/all_to_all | solution.py:153
  144.2 1.2 gather_fusion.3
  145.4 0.7 fusion.5
  146.2 1.3 copy.99
  147.5 0.6 reshape_reshape.17
  148.1 0.3 reshape_reshape.18
  148.4 5.6 %all_to_all.77 = f32[2,64,544]{2,1,0:T(8,128)S(1)} all-to-all(f32[2,64,544]{2,1,0:T(8,128)S(1)} %copy.101), channel_id=1, replica_groups=mesh['rows_0'=8,'rows_1'=8,'rows_2'=2,'rep'=4] {'rows_2'}, dimensions={0} | all-to-all | bytes 557056 | tf_op jit(solution)/shard_map/all_to_all | solution.py:43
  154.2 15.5 %all_to_all.78 = f32[64,1,544]{2,1,0:T(1,128)S(1)} all-to-all(f32[64,1,544]{2,1,0:T(1,128)S(1)} %all_to_all.58), channel_id=1, replica_groups=mesh['rows_0'=8,'rows_1'=8,'rows_2'=2,'rep'=4] {'rows_0','rows_1'}, dimensions={0} | all-to-all | bytes 278528 | tf_op jit(solution)/shard_map/all_to_all | solution.py:50
  169.7 0.1 reduce_sum.99
  169.8 0.7 broadcast_in_dim.162
  170.5 4.9 %all-to-all-start.9 = ((f32[64,1,544]{2,1,0:T(1,128)}), f32[64,1,544]{2,1,0:T(1,128)S(1)}, u32[]{:S(2)}, u32[]{:S(2)}) async-start(f32[64,1,544]{2,1,0:T(1,128)} %broadcast_in_dim.162), calls=%async_computation.9 | async-start | bytes 327680 | tf_op jit(solution)/shard_map/all_to_all | solution.py:19
  175.7 0.1 copy.106
  175.8 11.3 %all-to-all-done.9 = f32[64,1,544]{2,1,0:T(1,128)S(1)} async-done(((f32[64,1,544]{2,1,0:T(1,128)}), f32[64,1,544]{2,1,0:T(1,128)S(1)}, u32[]{:S(2)}, u32[]{:S(2)}) %all-to-all-start.9) | async-done | bytes 139296 | tf_op jit(solution)/shard_map/all_to_all | solution.py:19
  187.2 7.2 %all_to_all.79 = f32[2,64,544]{2,1,0:T(8,128)S(1)} all-to-all(f32[2,64,544]{2,1,0:T(8,128)S(1)} %broadcast_in_dim.164), channel_id=1, replica_groups=mesh['rows_0'=8,'rows_1'=8,'rows_2'=2,'rep'=4] {'rows_2'}, dimensions={0} | all-to-all | bytes 557056 | tf_op jit(solution)/shard_map/all_to_all | solution.py:19
  194.4 0.3 copy.102
  194.6 0.4 slice.34
  195.0 1.0 slice.32
  196.3 1.3 copy.108
  197.6 44.4 %gather_fusion.4 = f32[4096,16]{1,0:T(8,128)} fusion(f32[256,16,16]{2,1,0:T(8,128)S(1)} %copy.108, s32[4096]{0:T(1024)S(1)} %reshape.219), kind=kCustom, calls=%fused_computation.4 | custom fusion | bytes 557056 | tf_op jit(solution)/shard_map/gather | solution.py:203
  242.0 2.4 gather.35
  244.5 0.8 multiply_reduce_fusion
  245.2 0.6 broadcast_in_dim.168
  245.8 4.0 %all-to-all-start.11 = ((f32[4,1,256]{2,1,0:T(1,128)}), f32[4,1,256]{2,1,0:T(1,128)S(1)}, u32[]{:S(2)}, u32[]{:S(2)}) async-start(f32[4,1,256]{2,1,0:T(1,128)} %broadcast_in_dim.168), calls=%async_computation.11 | async-start | bytes 8192 | tf_op jit(solution)/shard_map/all_to_all | solution.py:19
  249.9 0.1 dynamic-slice_select_fusion
  250.0 0.7 copy.110
  250.7 3.3 %all-to-all-done.11 = f32[4,1,256]{2,1,0:T(1,128)S(1)} async-done(((f32[4,1,256]{2,1,0:T(1,128)}), f32[4,1,256]{2,1,0:T(1,128)S(1)}, u32[]{:S(2)}, u32[]{:S(2)}) %all-to-all-start.11) | async-done | bytes 4128 | tf_op jit(solution)/shard_map/all_to_all | solution.py:19
  254.0 0.6 broadcast_multiply_fusion
  (74 shorter events, 2.1 us)
Async XLA Ops:
  2.6 22.9 %copy-start.7 = (s32[256]{0:T(256)S(1)}, s32[256]{0:T(256)}, u32[]{:S(2)}) copy-start(s32[256]{0:T(256)} %param.9) | copy-start | bytes 3076
  2.7 23.3 %copy-start.5 = (s32[256]{0:T(256)S(1)}, s32[256]{0:T(256)}, u32[]{:S(2)}) copy-start(s32[256]{0:T(256)} %param.8) | copy-start | bytes 3076
  14.5 22.6 %all-to-all-start.1 = ((f32[64,1,514]{2,1,0:T(1,128)}), f32[64,1,514]{2,1,0:T(1,128)S(1)}, u32[]{:S(2)}, u32[]{:S(2)}) async-start(f32[64,1,514]{2,1,0:T(1,128)} %all_to_all.49), calls=%async_computation.1 | async-start | bytes 327680 | tf_op jit(solution)/shard_map/all_to_all | solution.py:50
  37.1 43.8 %copy-start.3 = (f32[256,256]{1,0:T(8,128)S(1)}, f32[256,256]{1,0:T(8,128)}, u32[]{:S(2)}) copy-start(f32[256,256]{1,0:T(8,128)} %param.11) | copy-start | bytes 786436
  37.1 19.4 %all-to-all-start.4 = ((s32[128,1,8]{2,1,0:T(1,128)}), s32[128,1,8]{2,1,0:T(1,128)S(1)}, u32[]{:S(2)}, u32[]{:S(2)}) async-start(s32[128,1,8]{2,1,0:T(1,128)} %bitcast.6), calls=%async_computation.4 | async-start | bytes 131072 | tf_op jit(solution)/shard_map/all_to_all | solution.py:119
  57.3 16.3 %all-to-all-start.2 = ((f32[64,1,514]{2,1,0:T(1,128)}), f32[64,1,514]{2,1,0:T(1,128)S(1)}, u32[]{:S(2)}, u32[]{:S(2)}) async-start(f32[64,1,514]{2,1,0:T(1,128)} %broadcast_in_dim.141), calls=%async_computation.2 | async-start | bytes 327680 | tf_op jit(solution)/shard_map/all_to_all | solution.py:19
  80.0 2.0 copy-start.2
  81.1 5.1 %copy-start.1 = (f32[256,256]{1,0:T(8,128)}, f32[256,256]{1,0:T(8,128)S(1)}, u32[]{:S(2)}) copy-start(f32[256,256]{1,0:T(8,128)S(1)} %fusion.10) | copy-start | bytes 786436
  86.2 26.3 %copy-start.8 = (f32[512,256]{1,0:T(8,128)S(1)}, f32[512,256]{1,0:T(8,128)}, u32[]{:S(2)}) copy-start(f32[512,256]{1,0:T(8,128)} %param.12) | copy-start | bytes 1572868
  87.2 25.3 %all-to-all-start.5 = ((bf16[128,8,256]{2,1,0:T(8,128)(2,1)}), bf16[128,8,256]{2,1,0:T(8,128)(2,1)S(1)}, u32[]{:S(2)}, u32[]{:S(2)}) async-start(bf16[128,8,256]{2,1,0:T(8,128)(2,1)} %bitcast_select_fusion.1), calls=%async_computation.5 | async-start | bytes 1048576 | tf_op jit(solution)/shard_map/all_to_all | solution.py:118
  113.0 3.5 %copy-start = (f32[512,256]{1,0:T(8,128)}, f32[512,256]{1,0:T(8,128)S(1)}, u32[]{:S(2)}) copy-start(f32[512,256]{1,0:T(8,128)S(1)} %fusion.4) | copy-start | bytes 1572868
  116.5 8.2 %copy-start.4 = (s32[256,16]{0,1:T(8,128)S(1)}, s32[256,16]{0,1:T(8,128)}, u32[]{:S(2)}) copy-start(s32[256,16]{0,1:T(8,128)} %param.10) | copy-start | bytes 49156
  117.5 26.7 %all-to-all-start.6 = ((bf16[128,8,256]{2,1,0:T(8,128)(2,1)}), bf16[128,8,256]{2,1,0:T(8,128)(2,1)S(1)}, u32[]{:S(2)}, u32[]{:S(2)}) async-start(bf16[128,8,256]{2,1,0:T(8,128)(2,1)} %fusion.7), calls=%async_computation.6 | async-start | bytes 1048576 | tf_op jit(solution)/shard_map/all_to_all | solution.py:153
  148.1 27.6 %copy-start.6 = (f32[2,256]{1,0:T(2,128)S(1)}, f32[2,256]{1,0:T(2,128)}, u32[]{:S(2)}) copy-start(f32[2,256]{1,0:T(2,128)} %param.13) | copy-start | bytes 6148
  170.5 16.6 %all-to-all-start.9 = ((f32[64,1,544]{2,1,0:T(1,128)}), f32[64,1,544]{2,1,0:T(1,128)S(1)}, u32[]{:S(2)}, u32[]{:S(2)}) async-start(f32[64,1,544]{2,1,0:T(1,128)} %broadcast_in_dim.162), calls=%async_computation.9 | async-start | bytes 327680 | tf_op jit(solution)/shard_map/all_to_all | solution.py:19
  245.8 8.1 %all-to-all-start.11 = ((f32[4,1,256]{2,1,0:T(1,128)}), f32[4,1,256]{2,1,0:T(1,128)S(1)}, u32[]{:S(2)}, u32[]{:S(2)}) async-start(f32[4,1,256]{2,1,0:T(1,128)} %broadcast_in_dim.168), calls=%async_computation.11 | async-start | bytes 8192 | tf_op jit(solution)/shard_map/all_to_all | solution.py:19
where the time goes:
time: 255 us
  waiting for transfers between devices  81.3 us (32%)
  local copies, waits for them, and re-layouts  72.5 us (28%)
  blocking collectives  45 us (18%)
  starting transfers between devices  45 us (18%)
  other arithmetic  7.18 us (3%)
    gather x2, local copies, waits for them, and re-layouts, shards(): book_view[pq_codes, jnp.arange(sub_dev, dtype=jnp.int32)[None, :]]  46.9 us
    all_to_all x3, waiting for transfers between devices, copy_for_each(): lax.all_to_all(jnp.broadcast_to(shard[None], (count, *shard.shape)), axis...  26.1 us
    all_to_all x1, waiting for transfers between devices, shards(): lax.all_to_all(at_owner.reshape(owner_rows, capacity, width_dev), ROWS, s...  18.7 us
    all_to_all x1, waiting for transfers between devices, shards(): lax.all_to_all(send_rows, ROWS, split_axis=0, concat_axis=0, tiled=True)  17.5 us
    all_to_all x2, blocking collectives, summed_on_arrival(): tiles = lax.all_to_all(cut_along(shard, dim, count), axis, 0, 0, tiled=True)  16.1 us
    all_to_all x1, blocking collectives, sum_in_two_steps(): return jnp.sum(lax.all_to_all(own, far, 0, 0, tiled=True), axis=0)  15.5 us
    all_to_all x3, starting transfers between devices, copy_for_each(): lax.all_to_all(jnp.broadcast_to(shard[None], (count, *shard.shape)), axis...  13.5 us
    all_to_all x2, blocking collectives, copy_for_each(): lax.all_to_all(jnp.broadcast_to(shard[None], (count, *shard.shape)), axis...  13.4 us
  transfers between devices with their start and end apart: 7, of which 7 were waited for; matrix products, arithmetic and copies ran while one was open for 3% of the time, Pallas kernels for 0%

commit v1 on v0

v1 whole, which is shorter than its diff:
```python
import functools

import jax
import jax.numpy as jnp
from jax import lax
from jax.experimental import pallas as pl
from jax.experimental.pallas import tpu as pltpu
from jax.sharding import Mesh
from jax.sharding import PartitionSpec as P

MESH = pl.DeviceIdType.MESH
ROWS = ("ry", "rz", "rc")
F32, BF16, I32 = jnp.float32, jnp.bfloat16, jnp.int32
LANES = 128


def iota(shape, dim):
    return lax.broadcasted_iota(I32, shape, dim)


def hot(cond):
    return jnp.where(cond, 1.0, 0.0).astype(BF16)


def dot(a, b):
    return jnp.dot(a, b, preferred_element_type=F32)


def parts(a, count):
    out = []
    for _ in range(count):
        p = a.astype(BF16)
        out.append(p)
        a = a - p.astype(F32)
    return out


def kernel(cfg, emb, cids, fids, pq, old_coarse, old_fine, old_book,
           o_coarse, o_fine, o_res, o_book, o_err,
           xs, xr, ms, mr, bs, br,
           in1, core1, rs1, x1, full1,
           in2, core2, rs2, x2, full2,
           err, s_send, s_x, s_m, s_b, s_ar1, s_ar2, s_e):
    Y, Z, C, X = cfg["Y"], cfg["Z"], cfg["C"], cfg["X"]
    R, n, W, cap, fine_dev, K, sub = (cfg[k] for k in ("R", "n", "W", "cap", "fine_dev", "K", "sub"))
    S, half, TR, sw = R * cap, K // 2, K // 2 // (Y + Z), W // sub
    groups = cfg["groups"]
    src_g, slots_g = R // groups, S // groups
    y, z, c, x = (lax.axis_index(a) for a in (*ROWS, "rep"))

    def at(dy=0, dz=0, dc=0, dx=0):
        return {
            "ry": lax.rem(y + dy, Y),
            "rz": lax.rem(z + dz, Z),
            "rc": lax.rem(c + dc, C),
            "rep": lax.rem(x + dx, X),
        }

    def offset(d):
        return at(d // (Z * C), lax.rem(d // C, Z), lax.rem(d, C))

    def back(d):
        dy, dz, dc = d // (Z * C), lax.rem(d // C, Z), lax.rem(d, C)
        return lax.rem(Y - dy, Y) * (Z * C) + lax.rem(Z - dz, Z) * C + lax.rem(C - dc, C)

    def remote(src, dst, recv, where, send):
        return pltpu.make_async_remote_copy(src, dst, send, recv, device_id=where, device_id_type=MESH)

    def arrived(ref, sem):
        pltpu.make_async_copy(ref, ref, sem).wait()

    gate = pltpu.get_barrier_semaphore()

    def greet(d, _):
        pl.semaphore_signal(gate, inc=1, device_id=offset(d), device_id_type=MESH)
        return 0

    lax.fori_loop(1, R, greet, 0)
    for d in range(1, X):
        pl.semaphore_signal(gate, inc=1, device_id=at(dx=d), device_id_type=MESH)

    cid_r, fid_r = cids[...], fids[...]
    own = fid_r // fine_dev
    loc = fid_r - own * fine_dev
    coarse_hot = hot(iota((K, n), 0) == cid_r)
    ones_lane = lambda lane: hot(iota((n, LANES), 1) == lane)
    pq16 = pq[...].astype(F32).astype(BF16)
    spread = hot((iota((sub, cap * sub), 1) & (sub - 1)) == iota((sub, cap * sub), 0))
    pq_wide = dot(pq16, spread)
    in1[:, :, :, :W] = dot(coarse_hot, emb[...]).reshape(2, Y + Z, TR, W)
    pq_rows = jnp.transpose(pq_wide[:, :LANES])
    tally = dot(coarse_hot, ones_lane(sub))
    for m in range(sub):
        tally += dot(hot(iota((K, n), 0).astype(F32) == pq_rows[m : m + 1, :]), ones_lane(m))
    in1[:, :, :, W:] = tally.reshape(2, Y + Z, TR, LANES)

    rel_r = (
        ((own // (Z * C) - y) & (Y - 1)) * (Z * C) + (((own // C) - z) & (Z - 1)) * C + ((own - c) & (C - 1))
    ).astype(F32)
    same = iota((n, n), 0) == iota((n, n), 1)

    def column(row):
        return jnp.sum(jnp.where(same, row, 0.0), axis=1, keepdims=True)

    rel_c, cid_c, loc_c = column(rel_r), column(cid_r.astype(F32)), column(loc.astype(F32))
    eq = rel_c == rel_r
    before = iota((n, n), 0) < iota((n, n), 1)
    after = iota((n, n), 0) > iota((n, n), 1)
    rank_r = jnp.sum(jnp.where(eq & before, 1.0, 0.0), axis=0, keepdims=True)
    rank_c = jnp.sum(jnp.where(eq & after, 1.0, 0.0), axis=1, keepdims=True)
    slot_r = rel_r * cap + rank_r
    slot_c = rel_c * cap + rank_c
    for g in range(groups):
        pick = hot((iota((slots_g, n), 0) + g * slots_g).astype(F32) == slot_r)
        rows = dot(pick, emb[...]).reshape(src_g, cap, W)
        xs[g * src_g : (g + 1) * src_g] = jnp.concatenate(
            [rows[:, :, w : w + LANES] for w in range(0, W, LANES)], axis=1
        ).astype(BF16)
    to_owner = hot(iota((R, n), 0).astype(F32) == rel_r)
    lane = iota((n, cap * sub), 1)
    slot_of_lane, field = (lane // sub).astype(F32), lane & (sub - 1)
    hi = jnp.floor(loc_c * (1.0 / 256.0))
    ids = jnp.where(field == 0, cid_c + 1.0, jnp.where(field == 1, loc_c - hi * 256.0, jnp.where(field == 2, hi + 1.0, 0.0)))
    mine = slot_of_lane == rank_c
    code_words = dot(to_owner, jnp.where(mine, pq_wide, 0.0).astype(BF16))
    id_words = dot(to_owner, jnp.where(mine, ids, 0.0).astype(BF16))
    ms[...] = jnp.concatenate([code_words, id_words], axis=1).reshape(R, 1, 2 * cap * sub)
    xr[0] = xs[0]
    mr[0] = ms[0]

    pl.semaphore_wait(gate, R - 1 + X - 1)

    def ar_core(inp, core, sems):
        remote(inp.at[1 - c], core, sems.at[0], at(dc=1), sems.at[8]).start()

    def ar_scatter(inp, core, rs, sems):
        arrived(core, sems.at[0])
        core[...] = core[...] + inp[c]
        for i in range(1, Y):
            remote(core.at[lax.rem(y + i, Y)], rs.at[0, i - 1], sems.at[1], at(dy=i), sems.at[9]).start()
        for i in range(1, Z):
            remote(core.at[Y + lax.rem(z + i, Z)], rs.at[1, i - 1], sems.at[2], at(dz=i), sems.at[10]).start()

    def ar_cross(core, rs, xx, sems):
        arrived(rs.at[0], sems.at[1])
        own_a = core[y] + jnp.sum(rs[0], axis=0)
        xx[0, z] = own_a
        for i in range(1, Z):
            remote(xx.at[0, z], xx.at[0, z], sems.at[3], at(dz=i), sems.at[11]).start()
        arrived(rs.at[1], sems.at[2])
        own_b = core[Y + z] + jnp.sum(rs[1], axis=0)
        xx[1, y] = own_b
        for i in range(1, Y):
            remote(xx.at[1, y], xx.at[1, y], sems.at[4], at(dy=i), sems.at[12]).start()

    def ar_gather(xx, full, sems, finish):
        arrived(rs_like(xx, Z), sems.at[3])
        full[c, y] = finish(jnp.sum(xx[0], axis=0), y)
        for i in range(1, Y):
            remote(full.at[c, y], full.at[c, y], sems.at[5], at(dy=i), sems.at[13]).start()
        arrived(rs_like(xx, Y), sems.at[4])
        full[c, Y + z] = finish(jnp.sum(xx[1], axis=0), Y + z)
        for i in range(1, Z):
            remote(full.at[c, Y + z], full.at[c, Y + z], sems.at[6], at(dz=i), sems.at[14]).start()

    def rs_like(xx, count):
        return xx.at[0, 0 : count - 1]

    def ar_pair(full, sems):
        arrived(full.at[0, 0 : Y - 1], sems.at[5])
        arrived(full.at[0, 0 : Z - 1], sems.at[6])
        remote(full.at[c], full.at[c], sems.at[7], at(dc=1), sems.at[15]).start()

    def ar_done(full, sems):
        arrived(full.at[0], sems.at[7])

    def ar_sent(inp, core, rs, xx, full, sems):
        arrived(core, sems.at[8])
        arrived(rs.at[0], sems.at[9])
        arrived(rs.at[1], sems.at[10])
        arrived(rs_like(xx, Z), sems.at[11])
        arrived(rs_like(xx, Y), sems.at[12])
        arrived(full.at[0, 0 : Y - 1], sems.at[13])
        arrived(full.at[0, 0 : Z - 1], sems.at[14])
        arrived(full.at[0], sems.at[15])

    def ship(g):
        def step(i, _):
            d = back(i)
            remote(xs.at[d], xr.at[i], s_x.at[g], offset_back(i), s_send.at[1]).start()
            return 0

        lax.fori_loop(max(1, g * src_g), (g + 1) * src_g, step, 0)

    def offset_back(i):
        return offset(back(i))

    def ship_words():
        def step(i, _):
            d = back(i)
            remote(ms.at[d], mr.at[i], s_m.at[0], offset_back(i), s_send.at[2]).start()
            return 0

        lax.fori_loop(1, R, step, 0)

    ar_core(in1, core1, s_ar1)
    ship(0)
    ar_scatter(in1, core1, rs1, s_ar1)
    ship_words()
    ar_cross(core1, rs1, x1, s_ar1)
    for g in range(1, groups // 2):
        ship(g)

    def coarse_mean(total, tile):
        first = pl.multiple_of(c * half + tile * TR, TR)
        count = total[:, W + sub : W + sub + 1]
        old = old_coarse[pl.ds(first, TR), :]
        mean = jnp.where(count > 0, total[:, :W] / jnp.maximum(count, 1.0), old)
        return jnp.concatenate([mean, total[:, W:]], axis=1)

    ar_gather(x1, full1, s_ar1, coarse_mean)
    for g in range(groups // 2, groups - 1):
        ship(g)
    ar_pair(full1, s_ar1)
    ship(groups - 1)

    def span(g):
        return slice(max(1, g * src_g), (g + 1) * src_g)

    arrived(mr.at[1:R], s_m.at[0])
    words = mr[...].reshape(R, 2 * cap * sub)
    code_w, id_w = words[:, : cap * sub], words[:, cap * sub :]
    by_src = hot((iota((S, R), 0) // cap) == iota((S, R), 1))
    mask_c = (iota((S, cap * sub), 1) // sub) == (iota((S, cap * sub), 0) & (cap - 1))
    pick_c = hot((iota((cap * sub, LANES), 0) & (sub - 1)) == iota((cap * sub, LANES), 1))
    id_c = dot(jnp.where(mask_c, dot(by_src, id_w.astype(BF16)), 0.0).astype(BF16), pick_c)
    by_src_t = hot((iota((R, S), 1) // cap) == iota((R, S), 0))
    mask_r = (iota((cap * sub, S), 0) // sub) == (iota((cap * sub, S), 1) & (cap - 1))
    pick_r = hot((iota((sub, cap * sub), 1) & (sub - 1)) == iota((sub, cap * sub), 0))

    def along_lanes(w):
        wide = dot(jnp.transpose(w).astype(BF16), by_src_t)
        return dot(pick_r, jnp.where(mask_r, wide, 0.0).astype(BF16))

    id_r, code_r = along_lanes(id_w), along_lanes(code_w)
    cid_slot = id_c[:, 0:1] - 1.0
    fid_slot = (id_c[:, 2:3] - 1.0) * 256.0 + id_c[:, 1:2]
    fid_lane = (id_r[2:3, :] - 1.0) * 256.0 + id_r[1:2, :]

    ar_done(full1, s_ar1)
    table = full1[...].reshape(K, W + LANES)
    o_coarse[...] = table[:, :W]
    coarse_parts = parts(table[:, :W], 3)

    fine_sum = jnp.zeros((fine_dev, W), F32)
    fine_count = jnp.zeros((fine_dev, 1), F32)
    for g in range(groups):
        arrived(xr.at[span(g)], s_x.at[g])
        lo = g * slots_g
        got = xr[g * src_g : (g + 1) * src_g].astype(F32)
        got = jnp.concatenate(
            [got[:, w * cap : (w + 1) * cap].reshape(slots_g, LANES) for w in range(W // LANES)], axis=1
        )
        c_hot = hot(iota((slots_g, K), 1).astype(F32) == cid_slot[lo : lo + slots_g])
        base = sum(dot(c_hot, p) for p in coarse_parts)
        cr = (got - base).astype(BF16)
        f_hot = iota((fine_dev, slots_g), 0).astype(F32) == fid_lane[:, lo : lo + slots_g]
        fine_sum += dot(hot(f_hot), cr)
        fine_count += jnp.sum(jnp.where(f_hot, 1.0, 0.0), axis=1, keepdims=True)
        cr_rows = cr.astype(F32).reshape(src_g, cap, W)
        xr[g * src_g : (g + 1) * src_g] = jnp.concatenate(
            [cr_rows[:, :, w : w + LANES] for w in range(0, W, LANES)], axis=1
        ).astype(BF16)
    new_fine = jnp.where(fine_count > 0, fine_sum / jnp.maximum(fine_count, 1.0), old_fine[...])
    o_fine[...] = new_fine
    fine_parts = parts(new_fine, 2)

    col = iota((1, W), 1) // sw
    code_sum = jnp.zeros((K, W), F32)
    for g in range(groups):
        lo = g * slots_g
        cr = xr[g * src_g : (g + 1) * src_g].astype(F32)
        cr = jnp.concatenate(
            [cr[:, w * cap : (w + 1) * cap].reshape(slots_g, LANES) for w in range(W // LANES)], axis=1
        )
        f_hot = hot(iota((slots_g, fine_dev), 1).astype(F32) == fid_slot[lo : lo + slots_g])
        res = (cr - sum(dot(f_hot, p) for p in fine_parts)).astype(BF16)
        res32 = res.astype(F32)
        res_rows = res32.reshape(src_g, cap, W)
        bs[g * src_g : (g + 1) * src_g] = jnp.concatenate(
            [res_rows[:, :, w : w + LANES] for w in range(0, W, LANES)], axis=1
        ).astype(BF16)

        def give(i, _):
            remote(bs.at[i], br.at[back(i)], s_b.at[0], offset(i), s_send.at[3]).start()
            return 0

        lax.fori_loop(max(1, g * src_g), (g + 1) * src_g, give, 0)
        for m in range(sub):
            k_hot = hot(iota((K, slots_g), 0).astype(F32) == code_r[m : m + 1, lo : lo + slots_g])
            code_sum += jnp.where(col == m, dot(k_hot, res), 0.0)
    in2[...] = code_sum.reshape(2, Y + Z, TR, W)
    br[0] = bs[0]

    counts = table[:, W:]
    widen = hot(iota((LANES, W), 1) // sw == iota((LANES, W), 0))
    count_wide = sum(dot(p, widen) for p in parts(counts, 2))

    ar_core(in2, core2, s_ar2)
    ar_scatter(in2, core2, rs2, s_ar2)
    ar_cross(core2, rs2, x2, s_ar2)
    ar_gather(x2, full2, s_ar2, lambda total, tile: total)
    ar_pair(full2, s_ar2)

    arrived(br.at[1:R], s_b.at[0])
    rows = br[...].astype(F32)
    rows = jnp.concatenate([rows[:, w * cap : (w + 1) * cap].reshape(S, LANES) for w in range(W // LANES)], axis=1)
    fetch = hot(iota((n, S), 1).astype(F32) == slot_c)
    res = dot(fetch, rows.astype(BF16))
    o_res[...] = res.astype(BF16)

    ar_done(full2, s_ar2)
    book = full2[...].reshape(K, W) / jnp.maximum(count_wide, 1.0)
    share = K // R
    me = (y * Z + z) * C + c
    tall = max(8, share)
    take = hot(iota((tall, K), 1) == iota((tall, K), 0) + me * share)
    own_book = sum(dot(take, p) for p in parts(book, 3))
    own_count = sum(dot(take, p) for p in parts(count_wide, 2))
    o_book[...] = jnp.where(own_count[:share] > 0, own_book[:share], old_book[...])
    book_parts = parts(book, 2)
    rebuilt = jnp.zeros((n, W), F32)
    for m in range(sub):
        k_hot = hot(iota((n, K), 1).astype(F32) == pq16[:, m : m + 1].astype(F32))
        rebuilt = jnp.where(col == m, sum(dot(k_hot, p) for p in book_parts), rebuilt)
    differ = res - rebuilt
    error = jnp.sum(differ * differ, axis=1, keepdims=True)
    error_row = jnp.sum(jnp.where(same, error, 0.0), axis=0, keepdims=True)
    err[x] = jnp.broadcast_to(error_row, (8, n))
    for d in range(1, X):
        remote(err.at[x], err.at[x], s_e.at[0], at(dx=d), s_send.at[4]).start()
    if X > 1:
        arrived(err.at[0 : X - 1], s_e.at[0])
    o_err[...] = jnp.sum(err[...], axis=0)[:1] * (1.0 / (W * X))

    if X > 1:
        arrived(err.at[0 : X - 1], s_send.at[4])
    arrived(xr.at[1:R], s_send.at[1])
    arrived(mr.at[1:R], s_send.at[2])
    arrived(br.at[1:R], s_send.at[3])
    ar_sent(in1, core1, rs1, x1, full1, s_ar1)
    ar_sent(in2, core2, rs2, x2, full2, s_ar2)


def shards(cfg, embeddings, coarse_ids, fine_ids, pq_codes, old_coarse, old_fine, old_codebook):
    n, W = embeddings.shape
    K, fine_dev, sub = old_coarse.shape[0], old_fine.shape[0], pq_codes.shape[1]
    Y, Z = cfg["Y"], cfg["Z"]
    R = Y * Z * cfg["C"]
    cap = 4 * n // R
    cfg = dict(cfg, R=R, n=n, W=W, cap=cap, fine_dev=fine_dev, K=K, sub=sub, groups=4)
    TR = K // 2 // (Y + Z)
    most = max(Y, Z)
    vm = pltpu.VMEM
    chunk = (R, cap * W // LANES, LANES)

    def ar(width):
        return [
            vm((2, Y + Z, TR, width), F32),
            vm((Y + Z, TR, width), F32),
            vm((2, most - 1, TR, width), F32),
            vm((2, most, TR, width), F32),
            vm((2, Y + Z, TR, width), F32),
        ]

    dma = pltpu.SemaphoreType.DMA
    outs = pl.pallas_call(
        functools.partial(kernel, cfg),
        out_shape=(
            jax.ShapeDtypeStruct((K, W), F32),
            jax.ShapeDtypeStruct((fine_dev, W), F32),
            jax.ShapeDtypeStruct((n, W), BF16),
            jax.ShapeDtypeStruct((K // R, W), F32),
            jax.ShapeDtypeStruct((1, n), F32),
        ),
        in_specs=[pl.BlockSpec(memory_space=vm)] * 7,
        out_specs=[pl.BlockSpec(memory_space=vm)] * 5,
        scratch_shapes=[
            vm(chunk, BF16),
            vm(chunk, BF16),
            vm((R, 1, 2 * cap * sub), F32),
            vm((R, 1, 2 * cap * sub), F32),
            vm(chunk, BF16),
            vm(chunk, BF16),
            *ar(W + LANES),
            *ar(W),
            vm((cfg["X"], 8, n), F32),
            dma((5,)),
            dma((4,)),
            dma((1,)),
            dma((1,)),
            dma((16,)),
            dma((16,)),
            dma((1,)),
        ],
        compiler_params=pltpu.CompilerParams(
            collective_id=0, has_side_effects=True, vmem_limit_bytes=48 * 2**20
        ),
    )(
        embeddings,
        coarse_ids.reshape(1, n),
        fine_ids.reshape(1, n),
        pq_codes,
        old_coarse,
        old_fine,
        old_codebook,
    )
    return (*outs[:4], outs[4].reshape(n))


def solution(mesh):
    devices = mesh.devices
    x = mesh.shape["rep"]
    chips = mesh.shape["rows"] // 2
    y = int(round(chips**0.5))
    z = chips // y
    torus = Mesh(devices.reshape(y, z, 2, x), (*ROWS, "rep"))
    cfg = {"Y": y, "Z": z, "C": 2, "X": x}
    return jax.shard_map(
        functools.partial(shards, cfg),
        mesh=torus,
        in_specs=(
            P(ROWS, "rep"),
            P(ROWS),
            P(ROWS),
            P(ROWS, "rep"),
            P(None, "rep"),
            P(ROWS, "rep"),
            P(ROWS, "rep"),
        ),
        out_specs=(P(None, "rep"), P(ROWS, "rep"), P(ROWS, "rep"), P(ROWS, "rep"), P(ROWS)),
        check_vma=False,
    )
```

time: 255 us -> 94.8 us (0.37)
  Pallas kernels: 0 us -> 87.7 us
  waiting for transfers between devices: 81.3 us -> 0 us
  local copies, waits for them, and re-layouts: 72.5 us -> 6.18 us
  blocking collectives: 45 us -> 0 us
  starting transfers between devices: 45 us -> 0 us
  other arithmetic: 7.18 us -> 0 us
    pallas_call x0 -> x1, Pallas kernels: none -> 87.7 us  [shards(): pl.pallas_call(functools.partial(kernel, cfg), out_shape=(jax.ShapeDtypeS...]
    all_to_all x7 -> x0, waiting for transfers between devices: 81.3 us -> none  [the longest x3 26.1 us: copy_for_each(): lax.all_to_all(jnp.broadcast_to(shard[None], (count, *shard.shape)), axis...]
    gather x7 -> x0, local copies, waits for them, and re-layouts: 56.5 us -> none  [the longest x2 46.9 us: shards(): book_view[pq_codes, jnp.arange(sub_dev, dtype=jnp.int32)[None, :]]]
    all_to_all x7 -> x0, starting transfers between devices: 45 us -> none  [the longest x3 13.5 us: copy_for_each(): lax.all_to_all(jnp.broadcast_to(shard[None], (count, *shard.shape)), axis...]
    all_to_all x5 -> x0, blocking collectives: 45 us -> none  [the longest x2 16.1 us: summed_on_arrival(): tiles = lax.all_to_all(cut_along(shard, dim, count), axis, 0, 0, tiled=True)]
    unnamed x25 -> x18, local copies, waits for them, and re-layouts: 1.14 us -> 6.18 us
    reduce_sum x10 -> x0, other arithmetic: 2.97 us -> none  [the longest x1 0.79 us: shards(): coarse_count = jnp.sum(coarse_hot, axis=1).astype(jnp.float32)]
    scatter x2 -> x0, local copies, waits for them, and re-layouts: 2.81 us -> none  [the longest x1 1.41 us: shards(): send_ids = jnp.full((slot_total,), -1, jnp.int32).at[slot_of_row].set(loc...]
  transfers between devices with their start and end apart: 7 -> 0, of which waited for: 7 -> 0; matrix products, arithmetic and copies ran while one was open for 3% -> 0% of each run, Pallas kernels for 0% -> 0%
where the time goes in v1:
time: 94.8 us; the launch traced here: 94.6 us
  Pallas kernels  87.7 us (93%)
  local copies, waits for them, and re-layouts  6.18 us (7%)
    pallas_call x1, Pallas kernels, shards(): pl.pallas_call(functools.partial(kernel, cfg), out_shape=(jax.ShapeDtypeS...  87.7 us
    unnamed x18, local copies, waits for them, and re-layouts  6.18 us

profile of v1, /device:TPU:1, one launch (start us, length us, event | category | flops | bytes accessed | tf_op | source)
XLA Modules:
  0.0 94.6 jit_solution(8715274893897742812)
XLA Ops:
  0.6 0.0 copy-start.2
  0.6 0.0 copy-start.3
  0.7 0.0 copy-start.4
  0.7 0.0 copy-start.5
  0.7 0.9 copy.12.pq
  1.6 0.0 copy-done.2
  1.6 0.0 copy-done.3
  1.6 0.0 copy-done.4
  1.6 0.0 copy-done.5
  1.6 0.0 copy-start
  1.6 1.0 %copy-done = f32[512,256]{1,0:T(8,128)S(1)} copy-done((f32[512,256]{1,0:T(8,128)S(1)}, f32[512,256]{1,0:T(8,128)}, u32[]{:S(2)}) %copy-start) | copy-done | bytes 524312
  2.6 0.0 copy-start.1
  2.6 0.9 %copy-done.1 = f32[256,256]{1,0:T(8,128)S(1)} copy-done((f32[256,256]{1,0:T(8,128)S(1)}, f32[256,256]{1,0:T(8,128)}, u32[]{:S(2)}) %copy-start.1) | copy-done | bytes 262168
  3.6 87.7 %shard_map.110 = (f32[256,256]{1,0:T(8,128)S(1)}, f32[512,256]{1,0:T(8,128)S(1)}, bf16[256,256]{1,0:T(8,128)(2,1)S(1)}, f32[2,256]{1,0:T(2,128)S(1)}, f32[1,256]{1,0:T(1,128)S(1)}) custom-call(bf16[256,256]{1,0:T(8,128)(2,1)S(1)} %copy-done.2, s32[1,256]{1,0:T(1,128)S(1)} %bitcast.4, s32[1,256]{1,0:T(1,128)S(1)} %bitcast.5, s32[256,16]{1,0:T(8,128)S(1)} %copy.12.pq, ...), custom_call_target="tpu_custom_call" | custom-call | tf_op jit(solution)/shard_map/pallas_call | solution.py:377
  91.3 0.7 copy.18
  92.0 0.8 copy.19
  92.8 0.7 copy.20
  93.5 0.6 copy.21
  94.1 0.6 copy.22
Async XLA Ops:
  0.6 0.9 copy-start.2
  0.6 0.9 copy-start.3
  0.7 0.9 copy-start.4
  0.7 0.9 copy-start.5
  1.6 1.0 %copy-start = (f32[512,256]{1,0:T(8,128)S(1)}, f32[512,256]{1,0:T(8,128)}, u32[]{:S(2)}) copy-start(f32[512,256]{1,0:T(8,128)} %old_fine.1) | copy-start | bytes 1572868
  2.6 0.9 %copy-start.1 = (f32[256,256]{1,0:T(8,128)S(1)}, f32[256,256]{1,0:T(8,128)}, u32[]{:S(2)}) copy-start(f32[256,256]{1,0:T(8,128)} %old_coarse.1) | copy-start | bytes 786436

commit v2 on v1

v2 whole, which is shorter than its diff:
```python
import functools

import jax
import jax.numpy as jnp
from jax import lax
from jax.experimental import pallas as pl
from jax.experimental.pallas import tpu as pltpu
from jax.sharding import Mesh
from jax.sharding import PartitionSpec as P

MESH = pl.DeviceIdType.MESH
ROWS = ("ry", "rz", "rc")
F32, BF16, I32 = jnp.float32, jnp.bfloat16, jnp.int32
LANES = 128


def iota(shape, dim):
    return lax.broadcasted_iota(I32, shape, dim)


def hot(cond):
    return jnp.where(cond, 1.0, 0.0).astype(BF16)


def dot(a, b):
    return jnp.dot(a, b, preferred_element_type=F32)


def parts(a, count):
    out = []
    for _ in range(count):
        p = a.astype(BF16)
        out.append(p)
        a = a - p.astype(F32)
    return out


def kernel(cfg, emb, cids, fids, pq_t, old_coarse, old_fine, old_book,
           o_coarse, o_fine, o_res, o_book, o_err,
           xs, xr, ms, mr, bs, br,
           in1, rs1, x1, full1,
           in2, rs2, x2, full2,
           err, held, coarse_old, fine_old, s_x, s_send, s_m, s_b, s_ar1, s_ar2, s_e, s_own):
    Y, Z, C, X = cfg["Y"], cfg["Z"], cfg["C"], cfg["X"]
    R, n, W, cap, fine_dev, K, sub = (cfg[k] for k in ("R", "n", "W", "cap", "fine_dev", "K", "sub"))
    S, half, TR, sw = R * cap, K // 2, K // 2 // (Y * C), W // sub
    groups = cfg["groups"]
    src_g, slots_g = R // groups, S // groups
    y, z, c, x = (lax.axis_index(a) for a in (*ROWS, "rep"))

    def at(dy=0, dz=0, dc=0, dx=0):
        return {
            "ry": (y + dy) & (Y - 1),
            "rz": (z + dz) & (Z - 1),
            "rc": (c + dc) & (C - 1),
            "rep": (x + dx) & (X - 1),
        }

    def peers(first, last, visit):
        def line(dy, skip=False):
            for dz in range(Z):
                for dc in range(C):
                    if not (skip and dz == 0 and dc == 0):
                        there = (dy * Z + dz) * C + dc
                        back = (((Y - dy) & (Y - 1)) * Z + (Z - dz) % Z) * C + (C - dc) % C
                        visit((dy, dz, dc), there, back)

        if first == 0:
            line(0, True)
            first = 1

        def step(dy, _):
            line(dy)
            return 0

        if last > first:
            lax.fori_loop(first, last, step, 0)

    def remote(src, dst, recv, where, send):
        return pltpu.make_async_remote_copy(src, dst, send, recv, device_id=where, device_id_type=MESH)

    def arrived(ref, sem):
        pltpu.make_async_copy(ref, ref, sem).wait()

    gate = pltpu.get_barrier_semaphore()

    def greet(off, there, back):
        pl.semaphore_signal(gate, inc=1, device_id=at(*off), device_id_type=MESH)

    peers(0, Y, greet)
    for d in range(1, X):
        pl.semaphore_signal(gate, inc=1, device_id=at(dx=d), device_id_type=MESH)

    tile_a, tile_b = y * C + c, z * C + c
    rows_a = pl.multiple_of(tile_a * TR, TR)
    rows_b = pl.multiple_of(half + tile_b * TR, TR)
    fetches = [
        pltpu.make_async_copy(old_coarse.at[pl.ds(rows_a, TR)], coarse_old.at[0], s_own.at[0]),
        pltpu.make_async_copy(old_coarse.at[pl.ds(rows_b, TR)], coarse_old.at[1], s_own.at[1]),
        pltpu.make_async_copy(old_fine, fine_old, s_own.at[2]),
    ]
    for f in fetches:
        f.start()

    cid_r, fid_r = cids[...], fids[...]
    own = fid_r // fine_dev
    loc = fid_r - own * fine_dev
    coarse_hot = hot(iota((K, n), 0) == cid_r)
    ones_lane = lambda lane: hot(iota((n, LANES), 1) == lane)
    pq_rows = pq_t[...].astype(F32)
    pq_tall = jnp.concatenate([pq_rows] * (LANES // sub), axis=0)
    pq16 = jnp.transpose(pq_tall)[:, :sub].astype(BF16)
    spread = hot((iota((sub, cap * sub), 1) & (sub - 1)) == iota((sub, cap * sub), 0))
    pq_wide = dot(pq16, spread)
    in1[:, :, :, :W] = dot(coarse_hot, emb[...]).reshape(2, Y * C, TR, W)
    tally = dot(coarse_hot, ones_lane(sub))
    for m in range(sub):
        tally += dot(hot(iota((K, n), 0).astype(F32) == pq_rows[m : m + 1, :]), ones_lane(m))
    in1[:, :, :, W:] = tally.reshape(2, Y * C, TR, LANES)

    rel_r = (
        ((own // (Z * C) - y) & (Y - 1)) * (Z * C) + (((own // C) - z) & (Z - 1)) * C + ((own - c) & (C - 1))
    ).astype(F32)
    same = iota((n, n), 0) == iota((n, n), 1)

    def column(row):
        return jnp.sum(jnp.where(same, row, 0.0), axis=1, keepdims=True)

    rel_c, cid_c, loc_c = column(rel_r), column(cid_r.astype(F32)), column(loc.astype(F32))
    eq = rel_c == rel_r
    before = iota((n, n), 0) < iota((n, n), 1)
    after = iota((n, n), 0) > iota((n, n), 1)
    rank_r = jnp.sum(jnp.where(eq & before, 1.0, 0.0), axis=0, keepdims=True)
    rank_c = jnp.sum(jnp.where(eq & after, 1.0, 0.0), axis=1, keepdims=True)
    slot_r = rel_r * cap + rank_r
    slot_c = rel_c * cap + rank_c
    for g in range(groups):
        pick = hot((iota((slots_g, n), 0) + g * slots_g).astype(F32) == slot_r)
        rows = dot(pick, emb[...]).reshape(src_g, cap, W)
        xs[g * src_g : (g + 1) * src_g] = jnp.concatenate(
            [rows[:, :, w : w + LANES] for w in range(0, W, LANES)], axis=1
        ).astype(BF16)
    to_owner = hot(iota((R, n), 0).astype(F32) == rel_r)
    lane = iota((n, cap * sub), 1)
    slot_of_lane, field = (lane // sub).astype(F32), lane & (sub - 1)
    hi = jnp.floor(loc_c * (1.0 / 256.0))
    ids = jnp.where(field == 0, cid_c + 1.0, jnp.where(field == 1, loc_c - hi * 256.0, jnp.where(field == 2, hi + 1.0, 0.0)))
    mine = slot_of_lane == rank_c
    code_words = dot(to_owner, jnp.where(mine, pq_wide, 0.0).astype(BF16))
    id_words = dot(to_owner, jnp.where(mine, ids, 0.0).astype(BF16))
    ms[...] = jnp.concatenate([code_words, id_words], axis=1).reshape(R, 1, 2 * cap * sub)
    xr[0] = xs[0]
    mr[0] = ms[0]

    pl.semaphore_wait(gate, R - 1 + X - 1)

    def line_peers(along):
        for i in range(1, (Z if along else Y) * C):
            d, dc = i // C, i % C
            yield i, ((at(dz=d, dc=dc), ((z + d) & (Z - 1)) * C + ((c + dc) & (C - 1))) if along else
                      (at(dy=d, dc=dc), ((y + d) & (Y - 1)) * C + ((c + dc) & (C - 1))))

    def ar_scatter(inp, rs, sems):
        for along in range(2):
            for i, (where, tile) in line_peers(along):
                remote(inp.at[along, tile], rs.at[along, i - 1], sems.at[along], where, sems.at[6 + along]).start()

    def ar_cross(inp, rs, xx, sems):
        for along, tile, place, count in ((0, tile_a, z, Z), (1, tile_b, y, Y)):
            arrived(rs.at[along], sems.at[along])
            xx[along, place] = inp[along, tile] + jnp.sum(rs[along], axis=0)
            for i in range(1, count):
                where = at(dy=i) if along else at(dz=i)
                remote(
                    xx.at[along, place], xx.at[along, place], sems.at[2 + along], where, sems.at[8 + along]
                ).start()

    def others(ref, along):
        return ref.at[along, 0 : (Y if along else Z) - 1]

    def line_of(full, along):
        return full.at[along, 0 : (Z if along else Y) * C - 1]

    def ar_gather(xx, full, sems, finish):
        for along, tile in ((0, tile_a), (1, tile_b)):
            arrived(others(xx, along), sems.at[2 + along])
            full[along, tile] = finish(jnp.sum(xx[along], axis=0), along)
            for i, (where, _) in line_peers(along):
                remote(
                    full.at[along, tile], full.at[along, tile], sems.at[4 + along], where, sems.at[10 + along]
                ).start()

    def ar_done(full, sems):
        for along in range(2):
            arrived(line_of(full, along), sems.at[4 + along])

    def ar_sent(rs, xx, full, sems):
        for along in range(2):
            arrived(rs.at[along], sems.at[6 + along])
            arrived(others(xx, along), sems.at[8 + along])
            arrived(line_of(full, along), sems.at[10 + along])

    per_group = Y // groups

    def ship(g):
        def visit(off, i, d):
            remote(xs.at[d], xr.at[i], s_x.at[g], at(-off[0], -off[1], -off[2]), s_send.at[0]).start()

        peers(g * per_group, (g + 1) * per_group, visit)

    def ship_words():
        def visit(off, i, d):
            remote(ms.at[d], mr.at[i], s_m.at[0], at(-off[0], -off[1], -off[2]), s_send.at[1]).start()

        peers(0, Y, visit)

    def give(g):
        def visit(off, i, d):
            remote(bs.at[i], br.at[d], s_b.at[0], at(*off), s_send.at[2]).start()

        peers(g * per_group, (g + 1) * per_group, visit)

    ar_scatter(in1, rs1, s_ar1)
    ship(0)
    ar_cross(in1, rs1, x1, s_ar1)
    ship(1)

    def coarse_mean(total, along):
        fetches[along].wait()
        count = total[:, W + sub : W + sub + 1]
        held[along] = total[:, W:]
        return jnp.where(count > 0, total[:, :W] / jnp.maximum(count, 1.0), coarse_old[along])

    ar_gather(x1, full1, s_ar1, coarse_mean)
    ship_words()
    for g in range(2, groups):
        ship(g)

    def span(g):
        return slice(max(1, g * src_g), (g + 1) * src_g)

    arrived(mr.at[1:R], s_m.at[0])
    words = mr[...].reshape(R, 2 * cap * sub)
    code_w, id_w = words[:, : cap * sub], words[:, cap * sub :]
    by_src = hot((iota((S, R), 0) // cap) == iota((S, R), 1))
    mask_c = (iota((S, cap * sub), 1) // sub) == (iota((S, cap * sub), 0) & (cap - 1))
    pick_c = hot((iota((cap * sub, LANES), 0) & (sub - 1)) == iota((cap * sub, LANES), 1))
    id_c = dot(jnp.where(mask_c, dot(by_src, id_w.astype(BF16)), 0.0).astype(BF16), pick_c)
    by_src_t = hot((iota((R, S), 1) // cap) == iota((R, S), 0))
    mask_r = (iota((cap * sub, S), 0) // sub) == (iota((cap * sub, S), 1) & (cap - 1))
    pick_r = hot((iota((sub, cap * sub), 1) & (sub - 1)) == iota((sub, cap * sub), 0))

    def along_lanes(w):
        wide = dot(jnp.transpose(w).astype(BF16), by_src_t)
        return dot(pick_r, jnp.where(mask_r, wide, 0.0).astype(BF16))

    id_r, code_r = along_lanes(id_w), along_lanes(code_w)
    cid_slot = id_c[:, 0:1] - 1.0
    fid_slot = (id_c[:, 2:3] - 1.0) * 256.0 + id_c[:, 1:2]
    fid_lane = (id_r[2:3, :] - 1.0) * 256.0 + id_r[1:2, :]

    ar_done(full1, s_ar1)
    table = full1[...].reshape(K, W)
    o_coarse[...] = table
    coarse_parts = parts(table, 3)

    fine_sum = jnp.zeros((fine_dev, W), F32)
    fine_count = jnp.zeros((fine_dev, 1), F32)
    for g in range(groups):
        arrived(xr.at[span(g)], s_x.at[g])
        lo = g * slots_g
        got = xr[g * src_g : (g + 1) * src_g].astype(F32)
        got = jnp.concatenate(
            [got[:, w * cap : (w + 1) * cap].reshape(slots_g, LANES) for w in range(W // LANES)], axis=1
        )
        c_hot = hot(iota((slots_g, K), 1).astype(F32) == cid_slot[lo : lo + slots_g])
        base = sum(dot(c_hot, p) for p in coarse_parts)
        cr = (got - base).astype(BF16)
        f_hot = iota((fine_dev, slots_g), 0).astype(F32) == fid_lane[:, lo : lo + slots_g]
        fine_sum += dot(hot(f_hot), cr)
        fine_count += jnp.sum(jnp.where(f_hot, 1.0, 0.0), axis=1, keepdims=True)
        cr_rows = cr.astype(F32).reshape(src_g, cap, W)
        xr[g * src_g : (g + 1) * src_g] = jnp.concatenate(
            [cr_rows[:, :, w : w + LANES] for w in range(0, W, LANES)], axis=1
        ).astype(BF16)
    fetches[2].wait()
    new_fine = jnp.where(fine_count > 0, fine_sum / jnp.maximum(fine_count, 1.0), fine_old[...])
    o_fine[...] = new_fine
    fine_parts = parts(new_fine, 2)

    col = iota((1, W), 1) // sw
    code_sum = jnp.zeros((K, W), F32)
    for g in range(groups):
        lo = g * slots_g
        cr = xr[g * src_g : (g + 1) * src_g].astype(F32)
        cr = jnp.concatenate(
            [cr[:, w * cap : (w + 1) * cap].reshape(slots_g, LANES) for w in range(W // LANES)], axis=1
        )
        f_hot = hot(iota((slots_g, fine_dev), 1).astype(F32) == fid_slot[lo : lo + slots_g])
        res = (cr - sum(dot(f_hot, p) for p in fine_parts)).astype(BF16)
        res32 = res.astype(F32)
        res_rows = res32.reshape(src_g, cap, W)
        bs[g * src_g : (g + 1) * src_g] = jnp.concatenate(
            [res_rows[:, :, w : w + LANES] for w in range(0, W, LANES)], axis=1
        ).astype(BF16)

        for m in range(sub):
            k_hot = hot(iota((K, slots_g), 0).astype(F32) == code_r[m : m + 1, lo : lo + slots_g])
            code_sum += jnp.where(col == m, dot(k_hot, res), 0.0)
    in2[...] = code_sum.reshape(2, Y * C, TR, W)
    br[0] = bs[0]

    widen = hot(iota((LANES, W), 1) // sw == iota((LANES, W), 0))
    none = 1e30

    def code_mean(total, along):
        count = sum(dot(p, widen) for p in parts(held[along], 2))
        return jnp.where(count > 0, total / jnp.maximum(count, 1.0), none)

    ar_scatter(in2, rs2, s_ar2)
    give(0)
    ar_cross(in2, rs2, x2, s_ar2)
    give(1)
    ar_gather(x2, full2, s_ar2, code_mean)
    for g in range(2, groups):
        give(g)

    arrived(br.at[1:R], s_b.at[0])
    rows = br[...].astype(F32)
    rows = jnp.concatenate([rows[:, w * cap : (w + 1) * cap].reshape(S, LANES) for w in range(W // LANES)], axis=1)
    fetch = hot(iota((n, S), 1).astype(F32) == slot_c)
    res = dot(fetch, rows.astype(BF16))
    o_res[...] = res.astype(BF16)

    ar_done(full2, s_ar2)
    book = full2[...].reshape(K, W)
    share = K // R
    me = (y * Z + z) * C + c
    tall = max(8, share)
    take = hot(iota((tall, K), 1) == iota((tall, K), 0) + me * share)
    own_book = sum(dot(take, p) for p in parts(book, 3))
    o_book[...] = jnp.where(own_book[:share] < 0.5 * none, own_book[:share], old_book[...])
    book_parts = parts(book, 2)
    rebuilt = jnp.zeros((n, W), F32)
    for m in range(sub):
        k_hot = hot(iota((n, K), 1).astype(F32) == pq16[:, m : m + 1].astype(F32))
        rebuilt = jnp.where(col == m, sum(dot(k_hot, p) for p in book_parts), rebuilt)
    differ = res - rebuilt
    error = jnp.sum(differ * differ, axis=1, keepdims=True)
    error_row = jnp.sum(jnp.where(same, error, 0.0), axis=0, keepdims=True)
    err[x] = jnp.broadcast_to(error_row, (8, n))
    for d in range(1, X):
        remote(err.at[x], err.at[x], s_e.at[0], at(dx=d), s_send.at[3]).start()
    if X > 1:
        arrived(err.at[0 : X - 1], s_e.at[0])
    o_err[...] = (jnp.sum(err[...], axis=0)[:1] * (1.0 / (W * X))).reshape(n)

    if X > 1:
        arrived(err.at[0 : X - 1], s_send.at[3])
    arrived(xr.at[1:R], s_send.at[0])
    arrived(mr.at[1:R], s_send.at[1])
    arrived(br.at[1:R], s_send.at[2])
    ar_sent(rs1, x1, full1, s_ar1)
    ar_sent(rs2, x2, full2, s_ar2)


def hand_over(*refs):
    count = (len(refs) - 1) // 2
    copies = [pltpu.make_async_copy(refs[i], refs[count + i], refs[-1].at[i]) for i in range(count)]
    for f in copies:
        f.start()
    for f in copies:
        f.wait()


def shards(cfg, embeddings, coarse_ids, fine_ids, pq_codes, old_coarse, old_fine, old_codebook):
    n, W = embeddings.shape
    K, fine_dev, sub = old_coarse.shape[0], old_fine.shape[0], pq_codes.shape[1]
    Y, Z = cfg["Y"], cfg["Z"]
    R = Y * Z * cfg["C"]
    cap = 4 * n // R
    cfg = dict(cfg, R=R, n=n, W=W, cap=cap, fine_dev=fine_dev, K=K, sub=sub, groups=min(4, Y))
    tiles = Y * cfg["C"]
    TR = K // 2 // tiles
    most = max(Y, Z)
    vm = pltpu.VMEM
    chunk = (R, cap * W // LANES, LANES)

    def ar(width):
        return [
            vm((2, tiles, TR, width), F32),
            vm((2, tiles - 1, TR, width), F32),
            vm((2, most, TR, width), F32),
            vm((2, tiles, TR, W), F32),
        ]

    dma = pltpu.SemaphoreType.DMA
    outs = pl.pallas_call(
        functools.partial(kernel, cfg),
        out_shape=(
            jax.ShapeDtypeStruct((K, W), F32),
            jax.ShapeDtypeStruct((fine_dev, W), F32),
            jax.ShapeDtypeStruct((n, W), BF16),
            jax.ShapeDtypeStruct((K // R, W), F32),
            jax.ShapeDtypeStruct((n,), F32),
        ),
        in_specs=[pl.BlockSpec(memory_space=vm)] * 4 + [pl.BlockSpec(memory_space=pl.ANY)] * 2 + [pl.BlockSpec(memory_space=vm)],
        out_specs=[pl.BlockSpec(memory_space=vm)] * 5,
        scratch_shapes=[
            vm(chunk, BF16),
            vm(chunk, BF16),
            vm((R, 1, 2 * cap * sub), F32),
            vm((R, 1, 2 * cap * sub), F32),
            vm(chunk, BF16),
            vm(chunk, BF16),
            *ar(W + LANES),
            *ar(W),
            vm((cfg["X"], 8, n), F32),
            vm((2, TR, LANES), F32),
            vm((2, TR, W), F32),
            vm((fine_dev, W), F32),
            dma((4,)),
            dma((4,)),
            dma((1,)),
            dma((1,)),
            dma((12,)),
            dma((12,)),
            dma((1,)),
            dma((3,)),
        ],
        compiler_params=pltpu.CompilerParams(
            collective_id=0, has_side_effects=True, vmem_limit_bytes=56 * 2**20
        ),
    )(
        embeddings,
        coarse_ids.reshape(1, n),
        fine_ids.reshape(1, n),
        pq_codes.T,
        old_coarse,
        old_fine,
        old_codebook,
    )
    return pl.pallas_call(
        hand_over,
        out_shape=tuple(jax.ShapeDtypeStruct(o.shape, o.dtype) for o in outs),
        in_specs=[pl.BlockSpec(memory_space=pl.ANY)] * 5,
        out_specs=[pl.BlockSpec(memory_space=pl.ANY)] * 5,
        scratch_shapes=[dma((5,))],
    )(*outs)


def solution(mesh):
    devices = mesh.devices
    x = mesh.shape["rep"]
    chips = mesh.shape["rows"] // 2
    y = int(round(chips**0.5))
    z = chips // y
    torus = Mesh(devices.reshape(y, z, 2, x), (*ROWS, "rep"))
    cfg = {"Y": y, "Z": z, "C": 2, "X": x}
    return jax.shard_map(
        functools.partial(shards, cfg),
        mesh=torus,
        in_specs=(
            P(ROWS, "rep"),
            P(ROWS),
            P(ROWS),
            P(ROWS, "rep"),
            P(None, "rep"),
            P(ROWS, "rep"),
            P(ROWS, "rep"),
        ),
        out_specs=(P(None, "rep"), P(ROWS, "rep"), P(ROWS, "rep"), P(ROWS, "rep"), P(ROWS)),
        check_vma=False,
    )
```

time: 94.8 us -> 123 us (1.30)
  Pallas kernels: 87.7 us -> 123 us
  local copies, waits for them, and re-layouts: 6.18 us -> 0 us
    pallas_call x0 -> x1, Pallas kernels: none -> 29 us  [shards(): pl.pallas_call(hand_over, out_shape=tuple((jax.ShapeDtypeStruct(o.shape,...]
    unnamed x18 -> x0, local copies, waits for them, and re-layouts: 6.18 us -> none
    pallas_call x1, Pallas kernels: 87.7 us -> 93.6 us  [shards(): pl.pallas_call(functools.partial(kernel, cfg), out_shape=(jax.ShapeDtypeS...]
where the time goes in v2:
time: 123 us
  Pallas kernels  123 us (100%)
    pallas_call x1, Pallas kernels, shards(): pl.pallas_call(functools.partial(kernel, cfg), out_shape=(jax.ShapeDtypeS...  93.6 us
    pallas_call x1, Pallas kernels, shards(): pl.pallas_call(hand_over, out_shape=tuple((jax.ShapeDtypeStruct(o.shape,...  29 us

profile of v2, /device:TPU:1, one launch (start us, length us, event | category | flops | bytes accessed | tf_op | source)
XLA Modules:
  0.0 123.3 jit_solution(11256901750893035893)
XLA Ops:
  0.6 93.6 %shard_map.110 = (f32[256,256]{1,0:T(8,128)}, f32[512,256]{1,0:T(8,128)}, bf16[256,256]{1,0:T(8,128)(2,1)}, f32[2,256]{1,0:T(2,128)}, f32[256]{0:T(256)}) custom-call(bf16[256,256]{1,0:T(8,128)(2,1)} %emb.1, s32[1,256]{1,0:T(1,128)} %bitcast.4, s32[1,256]{1,0:T(1,128)} %bitcast.5, s32[16,256]{1,0:T(8,128)} %bitcast.3, f32[256,256]{1,0:T(8,128)} %old_coarse.1, ...), custom_call_target="tpu_custom_call" | custom-call | tf_op jit(solution)/shard_map/pallas_call | solution.py:398
  94.3 29.0 %shard_map.111 = (f32[256,256]{1,0:T(8,128)}, f32[512,256]{1,0:T(8,128)}, bf16[256,256]{1,0:T(8,128)(2,1)}, f32[2,256]{1,0:T(2,128)}, f32[256]{0:T(256)}) custom-call(f32[256,256]{1,0:T(8,128)} %get-tuple-element.10.refs_0_, f32[512,256]{1,0:T(8,128)} %get-tuple-element.11.refs_1_, bf16[256,256]{1,0:T(8,128)(2,1)} %get-tuple-element.12.refs_2_, ...), custom_call_target="tpu_custom_call" | custom-call | tf_op jit(solution)/shard_map/pallas_call | solution.py:443

commit v3 on v1

--- a/solution.py
+++ b/solution.py
@@ -40,7 +40,7 @@
            xs, xr, ms, mr, bs, br,
            in1, core1, rs1, x1, full1,
            in2, core2, rs2, x2, full2,
-           err, s_send, s_x, s_m, s_b, s_ar1, s_ar2, s_e):
+           err, coarse_old, fine_old, s_own, s_send, s_x, s_m, s_b, s_ar1, s_ar2, s_e):
     Y, Z, C, X = cfg["Y"], cfg["Z"], cfg["C"], cfg["X"]
     R, n, W, cap, fine_dev, K, sub = (cfg[k] for k in ("R", "n", "W", "cap", "fine_dev", "K", "sub"))
     S, half, TR, sw = R * cap, K // 2, K // 2 // (Y + Z), W // sub
@@ -50,18 +50,36 @@
 
     def at(dy=0, dz=0, dc=0, dx=0):
         return {
-            "ry": lax.rem(y + dy, Y),
-            "rz": lax.rem(z + dz, Z),
-            "rc": lax.rem(c + dc, C),
-            "rep": lax.rem(x + dx, X),
+            "ry": (y + dy) & (Y - 1),
+            "rz": (z + dz) & (Z - 1),
+            "rc": (c + dc) & (C - 1),
+            "rep": (x + dx) & (X - 1),
         }
 
-    def offset(d):
-        return at(d // (Z * C), lax.rem(d // C, Z), lax.rem(d, C))
-
-    def back(d):
-        dy, dz, dc = d // (Z * C), lax.rem(d // C, Z), lax.rem(d, C)
-        return lax.rem(Y - dy, Y) * (Z * C) + lax.rem(Z - dz, Z) * C + lax.rem(C - dc, C)
+    zs = sorted(range(Z), key=lambda d: (min(d, Z - d), d))
+
+    def pair(k, visit):
+        first = isinstance(k, int) and k == 0
+        for dz in zs:
+            for dc in range(C):
+                for side in range(2):
+                    if first and side == dz == dc == 0:
+                        continue
+                    dy = (0, Y // 2)[side] if first else (k, Y - k)[side]
+                    other = side if first else 1 - side
+                    there = ((2 * k + side) * Z + dz) * C + dc
+                    back = ((2 * k + other) * Z + (Z - dz) % Z) * C + (C - dc) % C
+                    visit((dy, dz, dc), there, back)
+
+    def peers(visit):
+        pair(0, visit)
+
+        def step(k, _):
+            pair(k, visit)
+            return 0
+
+        if Y > 2:
+            lax.fori_loop(1, Y // 2, step, 0)
 
     def remote(src, dst, recv, where, send):
         return pltpu.make_async_remote_copy(src, dst, send, recv, device_id=where, device_id_type=MESH)
@@ -71,31 +89,39 @@
 
     gate = pltpu.get_barrier_semaphore()
 
-    def greet(d, _):
-        pl.semaphore_signal(gate, inc=1, device_id=offset(d), device_id_type=MESH)
-        return 0
-
-    lax.fori_loop(1, R, greet, 0)
+    def greet(off, there, back):
+        pl.semaphore_signal(gate, inc=1, device_id=at(*off), device_id_type=MESH)
+
+    peers(greet)
     for d in range(1, X):
         pl.semaphore_signal(gate, inc=1, device_id=at(dx=d), device_id_type=MESH)
+
+    fetches = [
+        pltpu.make_async_copy(old_coarse, coarse_old, s_own.at[0]),
+        pltpu.make_async_copy(old_fine, fine_old, s_own.at[1]),
+    ]
+    for f in fetches:
+        f.start()
 
     cid_r, fid_r = cids[...], fids[...]
     own = fid_r // fine_dev
     loc = fid_r - own * fine_dev
     coarse_hot = hot(iota((K, n), 0) == cid_r)
     ones_lane = lambda lane: hot(iota((n, LANES), 1) == lane)
-    pq16 = pq[...].astype(F32).astype(BF16)
+    pq_rows = pq[...].astype(F32)
+    pq16 = jnp.transpose(jnp.concatenate([pq_rows] * (LANES // sub), axis=0))[:, :sub].astype(BF16)
     spread = hot((iota((sub, cap * sub), 1) & (sub - 1)) == iota((sub, cap * sub), 0))
     pq_wide = dot(pq16, spread)
     in1[:, :, :, :W] = dot(coarse_hot, emb[...]).reshape(2, Y + Z, TR, W)
-    pq_rows = jnp.transpose(pq_wide[:, :LANES])
     tally = dot(coarse_hot, ones_lane(sub))
     for m in range(sub):
         tally += dot(hot(iota((K, n), 0).astype(F32) == pq_rows[m : m + 1, :]), ones_lane(m))
     in1[:, :, :, W:] = tally.reshape(2, Y + Z, TR, LANES)
 
+    turn = ((own // (Z * C)) - y) & (Y - 1)
+    place_y = jnp.where(turn == 0, 0, jnp.where(turn == Y // 2, 1, jnp.where(turn < Y // 2, 2 * turn, 2 * (Y - turn) + 1)))
     rel_r = (
-        ((own // (Z * C) - y) & (Y - 1)) * (Z * C) + (((own // C) - z) & (Z - 1)) * C + ((own - c) & (C - 1))
+        place_y * (Z * C) + (((own // C) - z) & (Z - 1)) * C + ((own - c) & (C - 1))
     ).astype(F32)
     same = iota((n, n), 0) == iota((n, n), 1)
 
@@ -185,23 +211,23 @@
         arrived(full.at[0], sems.at[15])
 
     def ship(g):
-        def step(i, _):
-            d = back(i)
-            remote(xs.at[d], xr.at[i], s_x.at[g], offset_back(i), s_send.at[1]).start()
-            return 0
-
-        lax.fori_loop(max(1, g * src_g), (g + 1) * src_g, step, 0)
-
-    def offset_back(i):
-        return offset(back(i))
+        def visit(off, i, d):
+            remote(xs.at[d], xr.at[i], s_x.at[g], at(-off[0], -off[1], -off[2]), s_send.at[1]).start()
+
+        pair(g, visit)
 
     def ship_words():
-        def step(i, _):
-            d = back(i)
-            remote(ms.at[d], mr.at[i], s_m.at[0], offset_back(i), s_send.at[2]).start()
-            return 0
-
-        lax.fori_loop(1, R, step, 0)
+        def visit(off, i, d):
+            remote(ms.at[d], mr.at[i], s_m.at[0], at(-off[0], -off[1], -off[2]), s_send.at[2]).start()
+
+        peers(visit)
+
+    def give(g):
+        def visit(off, i, d):
+            remote(bs.at[i], br.at[d], s_b.at[0], at(*off), s_send.at[3]).start()
+
+        if g < groups:
+            pair(g, visit)
 
     ar_core(in1, core1, s_ar1)
     ship(0)
@@ -211,10 +237,12 @@
     for g in range(1, groups // 2):
         ship(g)
 
+    fetches[0].wait()
+
     def coarse_mean(total, tile):
         first = pl.multiple_of(c * half + tile * TR, TR)
         count = total[:, W + sub : W + sub + 1]
-        old = old_coarse[pl.ds(first, TR), :]
+        old = coarse_old[pl.ds(first, TR), :]
         mean = jnp.where(count > 0, total[:, :W] / jnp.maximum(count, 1.0), old)
         return jnp.concatenate([mean, total[:, W:]], axis=1)
 
@@ -222,7 +250,8 @@
     for g in range(groups // 2, groups - 1):
         ship(g)
     ar_pair(full1, s_ar1)
-    ship(groups - 1)
+    if groups > 1:
+        ship(groups - 1)
 
     def span(g):
         return slice(max(1, g * src_g), (g + 1) * src_g)
@@ -271,7 +300,8 @@
         xr[g * src_g : (g + 1) * src_g] = jnp.concatenate(
             [cr_rows[:, :, w : w + LANES] for w in range(0, W, LANES)], axis=1
         ).astype(BF16)
-    new_fine = jnp.where(fine_count > 0, fine_sum / jnp.maximum(fine_count, 1.0), old_fine[...])
+    fetches[1].wait()
+    new_fine = jnp.where(fine_count > 0, fine_sum / jnp.maximum(fine_count, 1.0), fine_old[...])
     o_fine[...] = new_fine
     fine_parts = parts(new_fine, 2)
 
@@ -291,25 +321,24 @@
             [res_rows[:, :, w : w + LANES] for w in range(0, W, LANES)], axis=1
         ).astype(BF16)
 
-        def give(i, _):
-            remote(bs.at[i], br.at[back(i)], s_b.at[0], offset(i), s_send.at[3]).start()
-            return 0
-
-        lax.fori_loop(max(1, g * src_g), (g + 1) * src_g, give, 0)
         for m in range(sub):
             k_hot = hot(iota((K, slots_g), 0).astype(F32) == code_r[m : m + 1, lo : lo + slots_g])
             code_sum += jnp.where(col == m, dot(k_hot, res), 0.0)
     in2[...] = code_sum.reshape(2, Y + Z, TR, W)
+    ar_core(in2, core2, s_ar2)
     br[0] = bs[0]
 
     counts = table[:, W:]
     widen = hot(iota((LANES, W), 1) // sw == iota((LANES, W), 0))
     count_wide = sum(dot(p, widen) for p in parts(counts, 2))
 
-    ar_core(in2, core2, s_ar2)
+    give(0)
     ar_scatter(in2, core2, rs2, s_ar2)
+    give(1)
     ar_cross(core2, rs2, x2, s_ar2)
+    give(2)
     ar_gather(x2, full2, s_ar2, lambda total, tile: total)
+    give(3)
     ar_pair(full2, s_ar2)
 
     arrived(br.at[1:R], s_b.at[0])
@@ -341,7 +370,7 @@
         remote(err.at[x], err.at[x], s_e.at[0], at(dx=d), s_send.at[4]).start()
     if X > 1:
         arrived(err.at[0 : X - 1], s_e.at[0])
-    o_err[...] = jnp.sum(err[...], axis=0)[:1] * (1.0 / (W * X))
+    o_err[...] = (jnp.sum(err[...], axis=0)[:1] * (1.0 / (W * X))).reshape(n)
 
     if X > 1:
         arrived(err.at[0 : X - 1], s_send.at[4])
@@ -358,7 +387,7 @@
     Y, Z = cfg["Y"], cfg["Z"]
     R = Y * Z * cfg["C"]
     cap = 4 * n // R
-    cfg = dict(cfg, R=R, n=n, W=W, cap=cap, fine_dev=fine_dev, K=K, sub=sub, groups=4)
+    cfg = dict(cfg, R=R, n=n, W=W, cap=cap, fine_dev=fine_dev, K=K, sub=sub, groups=Y // 2)
     TR = K // 2 // (Y + Z)
     most = max(Y, Z)
     vm = pltpu.VMEM
@@ -381,9 +410,11 @@
             jax.ShapeDtypeStruct((fine_dev, W), F32),
             jax.ShapeDtypeStruct((n, W), BF16),
             jax.ShapeDtypeStruct((K // R, W), F32),
-            jax.ShapeDtypeStruct((1, n), F32),
+            jax.ShapeDtypeStruct((n,), F32),
         ),
-        in_specs=[pl.BlockSpec(memory_space=vm)] * 7,
+        in_specs=[pl.BlockSpec(memory_space=vm)] * 4
+        + [pl.BlockSpec(memory_space=pltpu.HBM)] * 2
+        + [pl.BlockSpec(memory_space=vm)],
         out_specs=[pl.BlockSpec(memory_space=vm)] * 5,
         scratch_shapes=[
             vm(chunk, BF16),
@@ -395,6 +426,9 @@
             *ar(W + LANES),
             *ar(W),
             vm((cfg["X"], 8, n), F32),
+            vm((K, W), F32),
+            vm((fine_dev, W), F32),
+            dma((2,)),
             dma((5,)),
             dma((4,)),
             dma((1,)),
@@ -404,18 +438,18 @@
             dma((1,)),
         ],
         compiler_params=pltpu.CompilerParams(
-            collective_id=0, has_side_effects=True, vmem_limit_bytes=48 * 2**20
+            collective_id=0, has_side_effects=True, vmem_limit_bytes=56 * 2**20
         ),
     )(
         embeddings,
         coarse_ids.reshape(1, n),
         fine_ids.reshape(1, n),
-        pq_codes,
+        pq_codes.T,
         old_coarse,
         old_fine,
         old_codebook,
     )
-    return (*outs[:4], outs[4].reshape(n))
+    return outs
 
 
 def solution(mesh):

time: 94.8 us -> 92.7 us (0.978)
  local copies, waits for them, and re-layouts: 6.18 us -> 4.65 us
    unnamed x18 -> x13, local copies, waits for them, and re-layouts: 6.18 us -> 4.65 us
where the time goes in v3:
time: 92.7 us; the launch traced here: 92.3 us
  Pallas kernels  87 us (94%)
  local copies, waits for them, and re-layouts  4.65 us (5%)
    pallas_call x1, Pallas kernels, shards(): pl.pallas_call(functools.partial(kernel, cfg), out_shape=(jax.ShapeDtypeS...  87 us
    unnamed x13, local copies, waits for them, and re-layouts  4.65 us

profile of v3, /device:TPU:1, one launch (start us, length us, event | category | flops | bytes accessed | tf_op | source)
XLA Modules:
  0.0 92.3 jit_solution(1690092702905158191)
XLA Ops:
  0.6 87.0 %shard_map.110 = (f32[256,256]{1,0:T(8,128)}, f32[512,256]{1,0:T(8,128)}, bf16[256,256]{1,0:T(8,128)(2,1)}, f32[2,256]{1,0:T(2,128)}, f32[256]{0:T(256)}) custom-call(bf16[256,256]{1,0:T(8,128)(2,1)} %emb.1, s32[1,256]{1,0:T(1,128)} %bitcast.4, s32[1,256]{1,0:T(1,128)} %bitcast.5, s32[16,256]{1,0:T(8,128)} %bitcast.3, f32[256,256]{1,0:T(8,128)} %old_coarse.1, ...), custom_call_target="tpu_custom_call" | custom-call | tf_op jit(solution)/shard_map/pallas_call | solution.py:406
  87.7 0.0 copy-start
  87.7 1.7 %copy.17 = f32[256,256]{1,0:T(8,128)} copy(f32[256,256]{1,0:T(8,128)} %get-tuple-element.10) | data formatting | bytes 524288
  89.4 0.0 copy-done
  89.4 0.0 copy-start.1
  89.4 0.8 copy.18
  90.2 0.2 copy-done.1
  90.4 0.0 copy-start.2
  90.4 0.7 copy.19
  91.1 0.0 copy-done.2
  91.1 0.0 copy-start.3
  91.1 0.6 copy.20
  91.7 0.1 copy-done.3
  91.8 0.6 copy.21
Async XLA Ops:
  87.7 1.7 %copy-start = (f32[512,256]{1,0:T(8,128)S(1)}, f32[512,256]{1,0:T(8,128)}, u32[]{:S(2)}) copy-start(f32[512,256]{1,0:T(8,128)} %get-tuple-element.11) | copy-start | bytes 1572868
  89.4 1.0 %copy-start.1 = (bf16[256,256]{1,0:T(8,128)(2,1)S(1)}, bf16[256,256]{1,0:T(8,128)(2,1)}, u32[]{:S(2)}) copy-start(bf16[256,256]{1,0:T(8,128)(2,1)} %get-tuple-element.12) | copy-start | bytes 393220
  90.4 0.7 copy-start.2
  91.1 0.7 copy-start.3

commit v4 on v3

--- a/solution.py
+++ b/solution.py
@@ -214,13 +214,15 @@
         def visit(off, i, d):
             remote(xs.at[d], xr.at[i], s_x.at[g], at(-off[0], -off[1], -off[2]), s_send.at[1]).start()
 
-        pair(g, visit)
-
-    def ship_words():
+        if g < groups:
+            pair(g, visit)
+
+    def ship_words(g):
         def visit(off, i, d):
             remote(ms.at[d], mr.at[i], s_m.at[0], at(-off[0], -off[1], -off[2]), s_send.at[2]).start()
 
-        peers(visit)
+        if g < groups:
+            pair(g, visit)
 
     def give(g):
         def visit(off, i, d):
@@ -232,11 +234,11 @@
     ar_core(in1, core1, s_ar1)
     ship(0)
     ar_scatter(in1, core1, rs1, s_ar1)
-    ship_words()
+    ship(1)
+    ship_words(0)
     ar_cross(core1, rs1, x1, s_ar1)
-    for g in range(1, groups // 2):
-        ship(g)
-
+    ship(2)
+    ship_words(1)
     fetches[0].wait()
 
     def coarse_mean(total, tile):
@@ -247,11 +249,10 @@
         return jnp.concatenate([mean, total[:, W:]], axis=1)
 
     ar_gather(x1, full1, s_ar1, coarse_mean)
-    for g in range(groups // 2, groups - 1):
-        ship(g)
+    ship(3)
+    ship_words(2)
     ar_pair(full1, s_ar1)
-    if groups > 1:
-        ship(groups - 1)
+    ship_words(3)
 
     def span(g):
         return slice(max(1, g * src_g), (g + 1) * src_g)

time: 92.7 us -> 95.2 us (1.027)
  Pallas kernels: 87 us -> 89.6 us
    pallas_call x1, Pallas kernels: 87 us -> 89.6 us  [shards(): pl.pallas_call(functools.partial(kernel, cfg), out_shape=(jax.ShapeDtypeS...]
where the time goes in v4:
time: 95.2 us; the launch traced here: 94.9 us
  Pallas kernels  89.6 us (94%)
  local copies, waits for them, and re-layouts  4.65 us (5%)
    pallas_call x1, Pallas kernels, shards(): pl.pallas_call(functools.partial(kernel, cfg), out_shape=(jax.ShapeDtypeS...  89.6 us
    unnamed x13, local copies, waits for them, and re-layouts  4.65 us

profile of v4, /device:TPU:1, one launch (start us, length us, event | category | flops | bytes accessed | tf_op | source)
XLA Modules:
  0.0 94.9 jit_solution(3474271078917681730)
XLA Ops:
  0.6 89.6 %shard_map.110 = (f32[256,256]{1,0:T(8,128)}, f32[512,256]{1,0:T(8,128)}, bf16[256,256]{1,0:T(8,128)(2,1)}, f32[2,256]{1,0:T(2,128)}, f32[256]{0:T(256)}) custom-call(bf16[256,256]{1,0:T(8,128)(2,1)} %emb.1, s32[1,256]{1,0:T(1,128)} %bitcast.4, s32[1,256]{1,0:T(1,128)} %bitcast.5, s32[16,256]{1,0:T(8,128)} %bitcast.3, f32[256,256]{1,0:T(8,128)} %old_coarse.1, ...), custom_call_target="tpu_custom_call" | custom-call | tf_op jit(solution)/shard_map/pallas_call | solution.py:407
  90.3 0.0 copy-start
  90.3 1.7 %copy.17 = f32[256,256]{1,0:T(8,128)} copy(f32[256,256]{1,0:T(8,128)} %get-tuple-element.10) | data formatting | bytes 524288
  92.0 0.0 copy-done
  92.0 0.0 copy-start.1
  92.0 0.8 copy.18
  92.8 0.2 copy-done.1
  93.0 0.0 copy-start.2
  93.0 0.7 copy.19
  93.7 0.0 copy-done.2
  93.7 0.0 copy-start.3
  93.7 0.6 copy.20
  94.3 0.1 copy-done.3
  94.4 0.6 copy.21
Async XLA Ops:
  90.3 1.7 %copy-start = (f32[512,256]{1,0:T(8,128)S(1)}, f32[512,256]{1,0:T(8,128)}, u32[]{:S(2)}) copy-start(f32[512,256]{1,0:T(8,128)} %get-tuple-element.11) | copy-start | bytes 1572868
  92.0 1.0 %copy-start.1 = (bf16[256,256]{1,0:T(8,128)(2,1)S(1)}, bf16[256,256]{1,0:T(8,128)(2,1)}, u32[]{:S(2)}) copy-start(bf16[256,256]{1,0:T(8,128)(2,1)} %get-tuple-element.12) | copy-start | bytes 393220
  93.0 0.7 copy-start.2
  93.7 0.7 copy-start.3
